TPU v7x, 256 devices: a whole 4x4x8 slice. The times are simulated.
256 devices in a mesh: seq: 64 (over x, z, y_lo), head: 4 (over y_hi, core).
Axes of the slice: x: 4, y: 4 (y_hi: 2, y_lo: 2; y = y_hi * 2 + y_lo), z: 8, core: 2. Of those that a mesh axis runs over, the one named last changes fastest.
Arguments:
- query_nope: bfloat16 [8192, 8192], P('seq', 'head'), may hold values from -6 to 6
- query_rope: bfloat16 [8192, 4096], P('seq', 'head'), may hold values from -6 to 6
- latent: bfloat16 [8192, 512], P('seq'), may hold values from -6 to 6
- key_rope: bfloat16 [8192, 64], P('seq'), may hold values from -6 to 6
- up_key: bfloat16 [512, 8192], P(None, 'head'), may hold values from -0.25 to 0.25
- up_value: bfloat16 [512, 8192], P(None, 'head'), may hold values from -0.25 to 0.25
- grad_out: bfloat16 [8192, 8192], P('seq', 'head'), may hold values from -6 to 6
- group_order: int32 [128], replicated, may hold values from 0 to 127, as said below
- tile_mask: int32 [128, 128], replicated, may hold values from 0 to 1, as said below
Outputs:
- output: bfloat16 [8192, 8192], P('seq', 'head')
- grad_query_nope: bfloat16 [8192, 8192], P('seq', 'head')
- grad_query_rope: bfloat16 [8192, 4096], P('seq', 'head')
- grad_latent: bfloat16 [8192, 512], P('seq')
- grad_key_rope: bfloat16 [8192, 64], P('seq')
Inputs may be any that keep to these rules, and one draw needn't show every extreme that they name: `group_order`: entries 2 d and 2 d + 1 name the groups of device d of seq, whose rows hold them in that order; the first is under 128 / 2 and the second is 127 minus the first; every group appears once. `tile_mask`: entry [a, b] is 1 exactly where group b does not come after group a and both lie in the same document; documents are runs of 1 to 8 consecutive groups, and the first document has exactly 8.
All inputs are finite; a program needn't handle non-finite values.
Results may differ from a plain program's by a relative error of at most 0.028.
Values may be sent and summed in bfloat16 or wider, within the bound.
A program may use at most 128 MiB of HBM per device.

v0:
```python
import jax
import jax.numpy as jnp
from jax import lax
from jax.sharding import PartitionSpec as P

HEAD_DEV = 16
LATENT = 512
ROPE = 64
NOPE = 128
DOC_GROUPS = 8


def window_product(left, right):
    return jnp.einsum("htc,kc->htk", left, right, preferred_element_type=jnp.float32)


def local(
    query_nope, query_rope, latent, key_rope, up_key, up_value, grad_out, group_order, tile_mask
):
    rows_local = latent.shape[0]
    group_rows = rows_local // 2
    width = LATENT + ROPE
    span = DOC_GROUPS
    score_scale = (NOPE + ROPE) ** (-0.5)
    device_index = lax.axis_index("seq")
    own_keys = jnp.concatenate([latent, key_rope], 1)
    key_rows = lax.all_gather(own_keys, "seq", axis=0, tiled=True)
    group_count = group_order.shape[0]
    key_blocks = key_rows.reshape(group_count, group_rows, width)
    blocks = jnp.arange(group_count, dtype=jnp.int32)
    own_groups = lax.dynamic_slice_in_dim(group_order, 2 * device_index, 2)
    weight_key = up_key.reshape(LATENT, HEAD_DEV, NOPE)
    weight_value = up_value.reshape(LATENT, HEAD_DEV, NOPE)
    offsets = jnp.arange(group_rows, dtype=jnp.int32)
    window_index = jnp.arange(span, dtype=jnp.int32)
    key_offset = jnp.tile(offsets, span)
    key_slot = jnp.repeat(window_index, group_rows, total_repeat_length=span * group_rows)
    causal = (key_slot[None, :] < span - 1) | (key_offset[None, :] <= offsets[:, None])
    outputs = []
    nope_grads = []
    rope_grads = []
    grad_full = jnp.zeros((group_count, group_rows, width), jnp.float32)
    for which in range(2):
        group_id = own_groups[which]
        near = group_id - (span - 1) + window_index
        clipped = jnp.maximum(near, 0)
        slots = jnp.sum(
            jnp.where(group_order[None, :] == clipped[:, None], blocks[None, :], 0), axis=1
        )
        tile_row = lax.dynamic_index_in_dim(tile_mask, group_id, 0, keepdims=False)
        picked = jnp.sum(
            jnp.where(blocks[None, :] == clipped[:, None], tile_row[None, :], 0), axis=1
        )
        live = (near >= 0) & (picked == 1)
        live_keys = jnp.repeat(live, group_rows, total_repeat_length=span * group_rows)
        allowed = (live_keys[None, :] & causal)[None, :, :]
        window = jnp.take(key_blocks, slots, axis=0).reshape(span * group_rows, width)
        latent_win = window[:, :LATENT]
        rows = slice(which * group_rows, (which + 1) * group_rows)
        query_part = query_nope[rows].reshape(group_rows, HEAD_DEV, NOPE)
        rope_part = query_rope[rows].reshape(group_rows, HEAD_DEV, ROPE)
        grad_part = grad_out[rows].reshape(group_rows, HEAD_DEV, NOPE)
        query_lat = jnp.einsum(
            "thd,chd->thc", query_part, weight_key, preferred_element_type=jnp.float32
        ).astype(jnp.bfloat16)
        query_full = jnp.concatenate([query_lat, rope_part], 2)
        query_heads = query_full.transpose(1, 0, 2)
        scores = window_product(query_heads, window) * score_scale
        row_top = jnp.max(jnp.where(allowed, scores, -1e30), axis=2, keepdims=True)
        weights = jnp.where(allowed, jnp.exp(scores - row_top), 0.0)
        normed = weights / jnp.sum(weights, axis=2, keepdims=True)
        normed_low = normed.astype(jnp.bfloat16)
        output_lat = jnp.einsum(
            "htk,kc->htc", normed_low, latent_win, preferred_element_type=jnp.float32
        )
        output_head = jnp.einsum(
            "htc,chd->thd",
            output_lat.astype(jnp.bfloat16),
            weight_value,
            preferred_element_type=jnp.float32,
        ).astype(jnp.bfloat16)
        grad_lat = jnp.einsum(
            "thd,chd->htc", grad_part, weight_value, preferred_element_type=jnp.float32
        )
        grad_lat_low = grad_lat.astype(jnp.bfloat16)
        row_delta = jnp.sum(grad_lat * output_lat, axis=2, keepdims=True)
        grad_prob = window_product(grad_lat_low, latent_win)
        grad_score = (normed * (grad_prob - row_delta)).astype(jnp.bfloat16)
        grad_query = (
            jnp.einsum("htk,kf->htf", grad_score, window, preferred_element_type=jnp.float32)
            * score_scale
        )
        grad_nope = jnp.einsum(
            "htc,chd->thd",
            grad_query[:, :, :LATENT].astype(jnp.bfloat16),
            weight_key,
            preferred_element_type=jnp.float32,
        ).astype(jnp.bfloat16)
        grad_rope = grad_query[:, :, LATENT:].astype(jnp.bfloat16).transpose(1, 0, 2)
        score_term = (
            jnp.einsum("htk,htf->kf", grad_score, query_heads, preferred_element_type=jnp.float32)
            * score_scale
        )
        value_term = jnp.einsum(
            "htk,htc->kc", normed_low, grad_lat_low, preferred_element_type=jnp.float32
        )
        term = (score_term + jnp.pad(value_term, ((0, 0), (0, ROPE)))).reshape(
            span, group_rows, width
        )
        grad_full = grad_full.at[slots].add(term)
        outputs.append(output_head.reshape(group_rows, HEAD_DEV * NOPE))
        nope_grads.append(grad_nope.reshape(group_rows, HEAD_DEV * NOPE))
        rope_grads.append(grad_rope.reshape(group_rows, HEAD_DEV * ROPE))
    output = jnp.concatenate(outputs, 0)
    grad_query_nope = jnp.concatenate(nope_grads, 0)
    grad_query_rope = jnp.concatenate(rope_grads, 0)
    grad_flat = grad_full.reshape(group_count * group_rows, width)
    reduced = lax.psum_scatter(grad_flat, "seq", scatter_dimension=0, tiled=True)
    grad_keys = lax.psum(reduced, "head").astype(jnp.bfloat16)
    return (output, grad_query_nope, grad_query_rope, grad_keys[:, :LATENT], grad_keys[:, LATENT:])


def solution(mesh):
    placed = (
        P("seq", "head"),
        P("seq", "head"),
        P("seq", None),
        P("seq", None),
        P(None, "head"),
        P(None, "head"),
        P("seq", "head"),
        P(),
        P(),
    )
    return jax.shard_map(
        local,
        mesh=mesh,
        in_specs=placed,
        out_specs=(
            P("seq", "head"),
            P("seq", "head"),
            P("seq", "head"),
            P("seq", None),
            P("seq", None),
        ),
        check_vma=False,
    )
```

profile of v0, /device:TPU:1, one launch (start us, length us, event | category | flops | bytes accessed | tf_op | source)
XLA Modules:
  0.0 870.2 jit_solution(185673542360179397)
XLA Ops:
  7.3 1.0 copy.59
  8.2 1.7 pad_maximum_fusion.3
  10.0 0.7 dynamic_slice.10
  10.7 0.6 fusion.126
  15.3 1.6 fusion.122
  16.9 1.1 reshape.347
  18.0 0.8 copy.58
  19.0 0.8 copy.65
  21.1 0.9 dynamic-slice_bitcast_fusion
  22.0 0.2 select_reduce_fusion.5
  22.2 0.7 fusion.124
  23.0 0.7 fusion.125
  23.7 0.7 fusion.123
  24.4 0.5 compare_and_fusion
  24.9 0.6 fusion.106
  25.5 10.2 %select_select_fusion.2 = (pred[512]{0:T(512)(128)(4,1)S(1)}, pred[512]{0:T(512)(128)(4,1)S(1)}) fusion(pred[]{:T(512)} %bitcast.10, pred[]{:T(512)} %bitcast.9, pred[]{:T(512)} %bitcast.8, pred[]{:T(512)} %bitcast.7, pred[]{:T(512)} %bitcast.6, pred[]{:T(512)} %bitcast.5, pred[]{:T(512)} %bitcast.4, pred[]{:T(512)} %bitcast.3, s32[4,128]{1,0:T(4,128)S(1)} %copy-done.14, ...), kind=kLoop, calls=%fused_computation.147 | loop fusion | flops 15872 | bytes 3104 | tf_op jit(solution)/shard_map/jit(_take)/select_n | solution.py:55
  35.7 4.5 compare_select_fusion.1
  40.2 0.7 fusion.105
  40.9 0.7 fusion.104
  41.6 0.7 slice_bitcast_fusion.9
  42.4 1.9 fusion.39
  44.3 1.8 fusion.36
  46.1 248.2 %all-gather.2.cloned.1.call-done = bf16[8192,576]{1,0:T(8,128)(2,1)} async-done(((bf16[128,576]{1,0:T(8,128)(2,1)}), bf16[8192,576]{1,0:T(8,128)(2,1)}) %all-gather.2.cloned.1.call-update) | async-done | bytes 9437200 | tf_op jit(solution)/shard_map/all_gather | solution.py:27
  294.3 4.6 gather_fusion.1
  299.0 5.4 gather_fusion
  304.6 2.5 fusion.86
  307.1 0.8 fusion.127
  307.9 0.8 fusion.93
  308.7 1.0 multiply_reduce_fusion
  309.7 0.3 copy-done.1
  310.0 0.8 convolution_bitcast_fusion.2
  310.9 0.8 multiply_convert_fusion.2
  311.7 1.0 copy-done.25
  312.7 1.8 fusion.33
  314.5 1.7 copy.82
  316.2 1.2 broadcast_select_fusion.1
  317.5 2.6 fusion.87
  320.0 0.8 fusion.128
  320.9 0.8 fusion.92
  321.9 1.0 multiply_reduce_fusion.1
  323.0 1.1 convolution_bitcast_fusion.3
  324.1 0.8 multiply_convert_fusion.3
  324.9 1.0 copy-done.27
  325.9 1.8 fusion.35
  327.7 2.8 copy.81
  330.6 9.6 %broadcast_in_dim.121 = f32[128,64,576]{2,1,0:T(8,128)} broadcast(f32[]{:T(128)} %constant.174.clone.1), dimensions={} | broadcast | bytes 18874372 | tf_op jit(solution)/shard_map/broadcast_in_dim | solution.py:42
  340.2 4.1 scatter_fusion
  344.3 3.7 scatter_fusion.1
  348.0 2.3 fusion.62
  350.4 1.0 multiply_convert_fusion
  351.4 0.5 copy-done.21
  351.9 0.6 fusion.68
  353.0 2.3 fusion.65
  355.4 1.0 multiply_convert_fusion.1
  356.3 0.5 copy-done.22
  356.9 0.6 fusion.71
  357.7 0.9 reshape.360
  358.6 1.6 pad_maximum_fusion.2
  360.2 0.8 pad_maximum_fusion
  361.0 0.8 pad_maximum_fusion.1
  361.9 480.3 %reduce-scatter.2.cloned.1.call-done = f32[128,576]{1,0:T(8,128)} async-done(((f32[8192,576]{1,0:T(8,128)}), f32[128,576]{1,0:T(8,128)}) %reduce-scatter.2.cloned.1.call-update) | async-done | bytes 294928 | tf_op jit(solution)/shard_map/reduce_scatter | solution.py:118
  842.2 19.8 %all-reduce.3 = bf16[128,576]{1,0:T(8,128)(2,1)S(1)} all-reduce(f32[128,576]{1,0:T(8,128)} %reduce-scatter.2.cloned.1.call-done), channel_id=1, replica_groups=mesh['seq'=64,'head'=4] {'head'}, use_global_device_ids=true, to_apply=%region_13.16 | all-reduce | flops 73728 | bytes 442368 | tf_op jit(solution)/shard_map/psum | solution.py:119
  862.0 0.7 slice.151
  862.7 0.7 copy.83
  (82 shorter events, 2.0 us)
Async XLA Ops:
  7.2 301.6 %copy-start = (bf16[512,2048]{1,0:T(8,128)(2,1)S(1)}, bf16[512,2048]{1,0:T(8,128)(2,1)}, u32[]{:S(2)}) copy-start(bf16[512,2048]{1,0:T(8,128)(2,1)} %param.24) | copy-start | bytes 6291460
  7.2 15.7 %copy-start.14 = (s32[4,128]{1,0:T(4,128)S(1)}, s32[4,128]{1,0:T(4,128)}, u32[]{:S(2)}) copy-start(s32[4,128]{1,0:T(4,128)} %constant.167.clone.1) | copy-start | bytes 6148
  7.2 14.8 %copy-start.19 = (s32[128]{0:T(128)S(1)}, s32[128]{0:T(128)}, u32[]{:S(2)}) copy-start(s32[128]{0:T(128)} %param.26) | copy-start | bytes 1540
  7.2 34.4 %copy-start.8 = (bf16[128,2048]{1,0:T(8,128)(2,1)S(1)}, bf16[128,2048]{1,0:T(8,128)(2,1)}, u32[]{:S(2)}) copy-start(bf16[128,2048]{1,0:T(8,128)(2,1)} %param.19) | copy-start | bytes 1572868
  7.2 287.1 %all-gather.2.cloned.1.call-start = ((), (), s32[]{:S(2)}) async-start(), calls=%async_computation.1 | async-start | bytes 10649600 | tf_op jit(solution)/shard_map/all_gather | solution.py:27
  8.2 33.4 %copy-start.9 = (bf16[128,2048]{1,0:T(8,128)(2,1)S(1)}, bf16[128,2048]{1,0:T(8,128)(2,1)}, u32[]{:S(2)}) copy-start(bf16[128,2048]{1,0:T(8,128)(2,1)} %param.25) | copy-start | bytes 1572868
  9.9 832.2 %reduce-scatter.2.cloned.1.call-start = ((), (), s32[]{:S(2)}) async-start(), calls=%async_computation.2 | async-start | bytes 21299200 | tf_op jit(solution)/shard_map/reduce_scatter | solution.py:118
  21.1 21.3 %copy-start.20 = (bf16[512,2048]{1,0:T(8,128)(2,1)S(1)}, bf16[512,2048]{1,0:T(8,128)(2,1)}, u32[]{:S(2)}) copy-start(bf16[512,2048]{1,0:T(8,128)(2,1)} %param.23) | copy-start | bytes 6291460
  46.1 258.3 %copy-start.18 = (pred[8]{0:T(512)(128)(4,1)S(1)}, pred[8]{0:T(512)(128)(4,1)}, u32[]{:S(2)}) copy-start(pred[8]{0:T(512)(128)(4,1)} %get-tuple-element.104) | copy-start | bytes 28
  46.1 258.5 %copy-start.11 = (bf16[64,16,64]{2,0,1:T(8,128)(2,1)S(1)}, bf16[64,16,64]{2,0,1:T(8,128)(2,1)}, u32[]{:S(2)}) copy-start(bf16[64,16,64]{2,0,1:T(8,128)(2,1)} %copy.65) | copy-start | bytes 393220
  304.6 6.3 copy-start.4
  304.6 2.5 copy-start.13
  308.7 1.3 copy-start.1
  310.9 1.8 copy-start.24
  311.7 1.0 copy-start.25
  314.5 1.7 copy-start.17
  317.5 6.6 copy-start.6
  317.5 2.6 copy-start.12
  320.9 1.0 copy-start.3
  321.7 1.3 copy-start.2
  324.1 1.8 copy-start.10
  324.1 1.8 copy-start.23
  324.9 1.0 copy-start.27
  330.6 9.6 %copy-start.16 = (s32[8]{0:T(128)S(1)}, s32[8]{0:T(128)}, u32[]{:S(2)}) copy-start(s32[8]{0:T(128)} %get-tuple-element.108) | copy-start | bytes 100
  340.2 4.1 copy-start.15
  347.9 2.4 copy-start.5
  348.0 2.4 copy-start.26
  350.3 1.6 copy-start.21
  352.9 2.4 copy-start.7
  352.9 2.4 copy-start.28
  355.3 1.6 copy-start.22
Sparse Core Ops, SparseCore 0:
  10.0 284.2 all-gather.1
  348.1 494.0 reduce-scatter.1
where the time goes:
time: 871 us; the launch traced here: 870 us
  waiting for transfers between devices  729 us (84%)
  local copies, waits for them, and re-layouts  41.6 us (5%)
  other arithmetic  33.2 us (4%)
  matrix products  27.1 us (3%)
  between operations  19.9 us (2%)
  blocking collectives  19.8 us (2%)
    reduce_scatter x1, waiting for transfers between devices, local(): lax.psum_scatter(grad_flat, 'seq', scatter_dimension=0, tiled=True)  480 us
    all_gather x1, waiting for transfers between devices, local(): key_rows = lax.all_gather(own_keys, 'seq', axis=0, tiled=True)  248 us
    psum x1, blocking collectives, local(): grad_keys = lax.psum(reduced, 'head').astype(jnp.bfloat16)  19.8 us
  transfers between devices with their start and end apart: 2, of which 2 were waited for; matrix products, arithmetic and copies ran while one was open for 5% of the time, Pallas kernels for 0%

commit v1 on v0

v1 whole, which is shorter than its diff:
```python
import functools
import math

import jax
import jax.numpy as jnp
from jax import lax
from jax.experimental import pallas as pl
from jax.experimental.pallas import tpu as pltpu
from jax.sharding import PartitionSpec as P

HEAD_DEV = 16
LATENT = 512
ROPE = 64
NOPE = 128
SPAN = 8
GROUP = 64
PAD = 128
WIDTH = PAD + LATENT
KEYS = SPAN * GROUP
ROWS = HEAD_DEV * GROUP
MESH = pl.DeviceIdType.MESH
SCALE = (NOPE + ROPE) ** (-0.5)
SCALE2 = SCALE * math.log2(math.e)
BLOCK = 256
F32 = jnp.float32
BF16 = jnp.bfloat16


def dot_nt(a, b):
    return lax.dot_general(a, b, (((1,), (1,)), ((), ())), preferred_element_type=F32)


def dot_nn(a, b):
    return lax.dot_general(a, b, (((1,), (0,)), ((), ())), preferred_element_type=F32)


def dot_tn(a, b):
    return lax.dot_general(a, b, (((0,), (0,)), ((), ())), preferred_element_type=F32)


def kernel(
    qn_hbm, qr_hbm, lat_ref, rope_ref, uk_hbm, uv_hbm, go_hbm, order_sm, order_row, mask_ref,
    out_hbm, gqn_hbm, gqr_hbm, glat_ref, grope_ref,
    qn, qr, uk, uv, gout, out_v, gqn_v, gqr_v,
    keyf, xbuf, send1, recv1, gather2, onehot, send2, window,
    qfull, glow, olat, gqlat, probs, dscore, bias,
    dwin, dsend, dpair, dmine, recvb, asum, apair, bsum, bpair, send4, recv4,
    insem, outsem, s1, s1x, r1, s1c, r1c, s2, s2x, r2, s2c, r2c,
    s3c, r3c, s4, s4x, r4, s5, r5, s6, r6, s7, s7x, r7, s7c, r7c,
):
    seq = lax.axis_index("seq")
    head = lax.axis_index("head")
    core = lax.rem(head, 2)
    parity = lax.rem(seq + core, 2)
    other = 1 - parity
    place = lax.div(seq, 2)
    half = lax.div(seq, 32)
    pair = lax.div(lax.rem(seq, 32), 2)
    seq_par = lax.rem(seq, 2)
    twin = (seq, head + 1 - 2 * core)
    far = (seq, lax.rem(head + 2, 4))

    def peer(o):
        return (2 * o + parity, head)

    loads = [
        pltpu.make_async_copy(src, dst, insem.at[n])
        for n, (src, dst) in enumerate(
            [(qn_hbm, qn), (qr_hbm, qr), (uk_hbm, uk), (uv_hbm, uv), (go_hbm, gout)]
        )
    ]
    for load in loads:
        load.start()

    barrier = pltpu.get_barrier_semaphore()

    def greet(i, carry):
        o = lax.rem(place + i, 32)
        pl.semaphore_signal(barrier, inc=1, device_id=peer(o), device_id_type=MESH)
        return carry

    lax.fori_loop(1, 32, greet, 0)

    @pl.when(core == 1)
    def _():
        pl.semaphore_signal(barrier, inc=1, device_id=peer(place), device_id_type=MESH)

    pl.semaphore_signal(barrier, inc=1, device_id=twin, device_id_type=MESH)
    pl.semaphore_signal(barrier, inc=1, device_id=far, device_id_type=MESH)

    lanes = lax.broadcasted_iota(jnp.int32, (128, PAD), 1)
    for b in range(4):
        keyf[b + 1] = lat_ref[:, b * 128:(b + 1) * 128].astype(F32)
    keyf[0] = jnp.concatenate([rope_ref[...].astype(F32), jnp.zeros((128, PAD - ROPE), F32)], 1)
    xbuf[...] = jnp.zeros_like(xbuf)
    for t in range(2):
        for q in range(2):
            for hf in range(2):
                for jb in range(3):
                    src = 0 if jb == 0 else hf * 2 + jb
                    xbuf[pl.ds(hf * 512 + (t * 2 + q) * 3 + jb, 32, stride=16), :] = keyf[
                        src, pl.ds(t * GROUP + q, 32, stride=2), :
                    ]
    send1[...] = xbuf[...].astype(BF16).reshape(64, 16, 128)
    recvb[...] = jnp.zeros_like(recvb)

    sub = lax.broadcasted_iota(jnp.int32, (8, 128), 0)
    row = jnp.broadcast_to(order_row[...], (8, 128))
    zero8 = jnp.zeros((8, 128), F32)

    def fill(n, carry):
        which = lax.div(n, 32)
        o = lax.rem(n, 32)
        group = order_sm[2 * (2 * o + parity) + which]
        hot = jnp.where(row == sub + (group - (SPAN - 1)), 1.0, 0.0).astype(F32)
        upper = jnp.concatenate([hot, zero8], 1)
        lower = jnp.concatenate([zero8, hot], 1)
        onehot[pl.ds(pl.multiple_of(n * 16, 16), 16), :] = jnp.concatenate([upper, lower], 0).astype(BF16)
        return carry

    lax.fori_loop(0, 64, fill, 0)

    @pl.when(core == 0)
    def _():
        pl.semaphore_wait(barrier, 33)

    @pl.when(core == 1)
    def _():
        pl.semaphore_wait(barrier, 34)

    def send_piece(src, dst_buf, sem_s, sem_r, o):
        pltpu.make_async_remote_copy(
            src_ref=src, dst_ref=dst_buf.at[seq_par, place], send_sem=sem_s, recv_sem=sem_r,
            device_id=peer(o), device_id_type=MESH,
        ).start()

    def phase1(i, carry):
        o = lax.rem(place + i, 32)
        send_piece(send1.at[2 * o + parity], recv1, s1, r1, o)
        return carry

    @pl.when(core == 0)
    def _():
        pltpu.make_async_copy(send1.at[seq], recv1.at[seq_par, place], r1).start()

    @pl.when(core == 1)
    def _():
        send_piece(send1.at[2 * place + parity], recv1, s1x, r1, place)

    lax.fori_loop(1, 32, phase1, 0)
    pltpu.make_async_copy(recv1.at[parity], recv1.at[parity], r1).wait()
    cross1 = pltpu.make_async_remote_copy(
        src_ref=recv1.at[parity], dst_ref=recv1.at[parity], send_sem=s1c, recv_sem=r1c,
        device_id=twin, device_id_type=MESH,
    )
    cross1.start()
    pltpu.make_async_copy(recv1.at[other], recv1.at[other], r1c).wait()

    xbuf[...] = recv1[...].reshape(1024, 128).astype(F32)
    for q in range(2):
        for t in range(2):
            for jb in range(3):
                gather2[(q * 2 + t) * 64:(q * 2 + t + 1) * 64, jb * 128:(jb + 1) * 128] = xbuf[
                    pl.ds((t * 2 + q) * 3 + jb, 64, stride=16), :
                ].astype(BF16)

    def send_window(which, o, sem_s):
        @pl.when(half == 0)
        def _():
            pltpu.make_async_remote_copy(
                src_ref=send2.at[which, o], dst_ref=window.at[which, pair, seq_par, :, pl.ds(0, 384)],
                send_sem=sem_s, recv_sem=r2.at[which], device_id=peer(o), device_id_type=MESH,
            ).start()

        @pl.when(half == 1)
        def _():
            pltpu.make_async_remote_copy(
                src_ref=send2.at[which, o, :, pl.ds(128, 256)],
                dst_ref=window.at[which, pair, seq_par, :, pl.ds(384, 256)],
                send_sem=sem_s, recv_sem=r2.at[which], device_id=peer(o), device_id_type=MESH,
            ).start()

    for which in range(2):
        picked = dot_nn(onehot[which * 512:(which + 1) * 512, :], gather2[...])
        send2[which] = picked.astype(BF16).reshape(32, 16, 384)

        @pl.when(core == 0)
        def _():
            @pl.when(half == 0)
            def _():
                pltpu.make_async_copy(
                    send2.at[which, place], window.at[which, pair, seq_par, :, pl.ds(0, 384)], r2.at[which]
                ).start()

            @pl.when(half == 1)
            def _():
                pltpu.make_async_copy(
                    send2.at[which, place, :, pl.ds(128, 256)],
                    window.at[which, pair, seq_par, :, pl.ds(384, 256)], r2.at[which],
                ).start()

        @pl.when(core == 1)
        def _():
            send_window(which, place, s2x.at[which])

        def phase2(i, carry):
            send_window(which, lax.rem(place + i, 32), s2.at[which])
            return carry

        lax.fori_loop(1, 32, phase2, 0)

    for load in loads:
        load.wait()

    def project(h, carry):
        cols = pl.ds(pl.multiple_of(h * NOPE, NOPE), NOPE)
        rows = pl.ds(pl.multiple_of(h * GROUP, GROUP), GROUP)
        ql = dot_nt(qn[:, cols], uk[:, cols]).astype(BF16)
        gl = dot_nt(gout[:, cols], uv[:, cols]).astype(BF16)
        for w in range(2):
            qfull[w, rows, pl.ds(PAD, LATENT)] = ql[w * GROUP:(w + 1) * GROUP]
            glow[w, rows, :] = gl[w * GROUP:(w + 1) * GROUP]
        return carry

    lax.fori_loop(0, HEAD_DEV, project, 0)

    def rotary(m, carry):
        two = qr[:, pl.ds(pl.multiple_of(m * 128, 128), 128)].astype(F32)
        even = jnp.where(lanes < ROPE, two, 0.0).astype(BF16)
        odd = jnp.where(lanes < ROPE, pltpu.roll(two, ROPE, 1), 0.0).astype(BF16)
        for w in range(2):
            qfull[w, pl.ds(pl.multiple_of(m * 128, 128), GROUP), pl.ds(0, PAD)] = even[w * GROUP:(w + 1) * GROUP]
            qfull[w, pl.ds(pl.multiple_of(m * 128 + GROUP, GROUP), GROUP), pl.ds(0, PAD)] = odd[
                w * GROUP:(w + 1) * GROUP
            ]
        return carry

    lax.fori_loop(0, HEAD_DEV // 2, rotary, 0)

    col = lax.broadcasted_iota(jnp.int32, (GROUP, KEYS), 1)
    slot = lax.rem(col, SPAN)
    key_row = lax.div(col, SPAN)
    query_row = lax.broadcasted_iota(jnp.int32, (GROUP, KEYS), 0)
    for which in range(2):
        group = order_sm[2 * seq + which]
        seen = jnp.sum(mask_ref[pl.ds(group, 1), :], axis=1, keepdims=True)
        allowed = (slot >= SPAN - seen) & ((slot < SPAN - 1) | (key_row <= query_row))
        bias[which] = jnp.where(allowed, 0.0, -1e30).astype(F32)

    def send_grad(which, o, sem_s):
        dst = lax.div(o, 2)
        hf = lax.div(o, 16)

        @pl.when(hf == 0)
        def _():
            pltpu.make_async_remote_copy(
                src_ref=dmine.at[which, lax.rem(o, 16), :, pl.ds(0, 384)], dst_ref=recvb.at[which, place],
                send_sem=sem_s, recv_sem=r4.at[which], device_id=peer(o), device_id_type=MESH,
            ).start()

        @pl.when(hf == 1)
        def _():
            pltpu.make_async_remote_copy(
                src_ref=dmine.at[which, lax.rem(o, 16), :, pl.ds(384, 256)],
                dst_ref=recvb.at[which, place, :, pl.ds(128, 256)],
                send_sem=sem_s, recv_sem=r4.at[which], device_id=peer(o), device_id_type=MESH,
            ).start()

    cross2 = []
    for which in range(2):
        pltpu.make_async_copy(window.at[which, :, parity], window.at[which, :, parity], r2.at[which]).wait()
        cross2.append(pltpu.make_async_remote_copy(
            src_ref=window.at[which, :, parity], dst_ref=window.at[which, :, parity],
            send_sem=s2c.at[which], recv_sem=r2c.at[which], device_id=twin, device_id_type=MESH,
        ))
        cross2[which].start()
        pltpu.make_async_copy(window.at[which, :, other], window.at[which, :, other], r2c.at[which]).wait()

        def attend(n, carry):
            rows = pl.ds(pl.multiple_of(n * BLOCK, BLOCK), BLOCK)
            keys = window[which].reshape(KEYS, WIDTH)
            lat = keys[:, PAD:]
            scores = dot_nt(qfull[which, rows, :], keys) * SCALE2
            scores = (scores.reshape(BLOCK // GROUP, GROUP, KEYS) + bias[which][None]).reshape(BLOCK, KEYS)
            top = jnp.max(scores, axis=1, keepdims=True)
            weights = jnp.exp2(scores - top)
            normed = weights * (1.0 / jnp.sum(weights, axis=1, keepdims=True))
            low = normed.astype(BF16)
            grad_prob = dot_nt(glow[which, rows, :], lat)
            prod = normed * grad_prob
            delta = jnp.sum(prod, axis=1, keepdims=True)
            ds = (prod - normed * delta).astype(BF16)
            probs[rows, :] = low
            dscore[rows, :] = ds
            ol = dot_nn(low, lat).astype(BF16)
            gq = (dot_nn(ds, keys) * SCALE).astype(BF16)
            for j in range(BLOCK // GROUP):
                piece = slice(j * GROUP, (j + 1) * GROUP)
                olat[n * (BLOCK // GROUP) + j, which * GROUP:(which + 1) * GROUP, :] = ol[piece]
                gqlat[n * (BLOCK // GROUP) + j, which * GROUP:(which + 1) * GROUP, :] = gq[piece, PAD:]
            for j in range(0, BLOCK // GROUP, 2):
                two = jnp.concatenate(
                    [gq[j * GROUP:(j + 1) * GROUP, :ROPE], gq[(j + 1) * GROUP:(j + 2) * GROUP, :ROPE]], 1
                )
                gqr_v[
                    which * GROUP:(which + 1) * GROUP,
                    pl.ds(pl.multiple_of(n * (BLOCK // 2 * 2) + j * ROPE, 128), 128),
                ] = two
            return carry

        lax.fori_loop(0, ROWS // BLOCK, attend, 0)

        def key_grad(n, carry):
            krows = pl.ds(pl.multiple_of(n * 256, 256), 256)
            first = dot_tn(dscore[:, krows], qfull[which]) * SCALE
            second = dot_tn(probs[:, krows], glow[which])
            total = jnp.concatenate([first[:, :PAD], first[:, PAD:] + second], 1)
            dwin[which, pl.ds(n * 8, 8)] = total.reshape(8, 2, 16, WIDTH)
            return carry

        lax.fori_loop(0, KEYS // 256, key_grad, 0)

        dsend[which] = dwin[which, :, other].astype(BF16)
        cross3 = pltpu.make_async_remote_copy(
            src_ref=dsend.at[which], dst_ref=dpair.at[which], send_sem=s3c.at[which], recv_sem=r3c.at[which],
            device_id=twin, device_id_type=MESH,
        )
        cross3.start()
        cross3.wait_recv()
        dmine[which] = (dwin[which, :, parity] + dpair[which].astype(F32)).astype(BF16)

        @pl.when(core == 0)
        def _():
            @pl.when(half == 0)
            def _():
                pltpu.make_async_copy(
                    dmine.at[which, lax.rem(place, 16), :, pl.ds(0, 384)], recvb.at[which, place], r4.at[which]
                ).start()

            @pl.when(half == 1)
            def _():
                pltpu.make_async_copy(
                    dmine.at[which, lax.rem(place, 16), :, pl.ds(384, 256)],
                    recvb.at[which, place, :, pl.ds(128, 256)], r4.at[which],
                ).start()

        @pl.when(core == 1)
        def _():
            send_grad(which, place, s4x.at[which])

        def phase4(i, carry):
            send_grad(which, lax.rem(place + i, 32), s4.at[which])
            return carry

        lax.fori_loop(1, 32, phase4, 0)

    def unproject(h, carry):
        cols = pl.ds(pl.multiple_of(h * NOPE, NOPE), NOPE)
        out_v[:, cols] = dot_nn(olat[h], uv[:, cols]).astype(BF16)
        gqn_v[:, cols] = dot_nn(gqlat[h], uk[:, cols]).astype(BF16)
        return carry

    lax.fori_loop(0, HEAD_DEV, unproject, 0)
    stores = [
        pltpu.make_async_copy(src, dst, outsem.at[n])
        for n, (src, dst) in enumerate([(out_v, out_hbm), (gqn_v, gqn_hbm), (gqr_v, gqr_hbm)])
    ]
    for store in stores:
        store.start()

    total = jnp.zeros((256, 384), F32)
    for which in range(2):
        @pl.when(half == 0)
        def _():
            pltpu.make_async_copy(recvb.at[which], recvb.at[which], r4.at[which]).wait()

        @pl.when(half == 1)
        def _():
            ref = recvb.at[which, :, :, pl.ds(128, 256)]
            pltpu.make_async_copy(ref, ref, r4.at[which]).wait()

        total = total + dot_tn(onehot[which * 512:(which + 1) * 512, :], recvb[which].reshape(512, 384))
    asum[...] = total.reshape(4, 2, 32, 384)
    cross5 = pltpu.make_async_remote_copy(
        src_ref=asum.at[:, other], dst_ref=apair, send_sem=s5, recv_sem=r5, device_id=twin, device_id_type=MESH,
    )
    cross5.start()
    cross5.wait_recv()
    bsum[...] = asum[:, parity] + apair[...]
    cross6 = pltpu.make_async_remote_copy(
        src_ref=bsum, dst_ref=bpair, send_sem=s6, recv_sem=r6, device_id=far, device_id_type=MESH,
    )
    cross6.start()
    cross6.wait_recv()

    for q in range(2):
        for t in range(2):
            final = bsum[q * 2 + t] + bpair[q * 2 + t]
            for jb in range(3):
                xbuf[pl.ds((t * 2 + q) * 3 + jb, 32, stride=16), :] = final[:, jb * 128:(jb + 1) * 128]
    send4[...] = xbuf[pl.ds(0, 512), :].astype(BF16).reshape(32, 16, 128)

    @pl.when(core == 0)
    def _():
        pltpu.make_async_copy(send4.at[place], recv4.at[seq_par, place], r7).start()

    @pl.when(core == 1)
    def _():
        send_piece(send4.at[place], recv4, s7x, r7, place)

    def phase7(i, carry):
        o = lax.rem(place + i, 32)
        send_piece(send4.at[o], recv4, s7, r7, o)
        return carry

    lax.fori_loop(1, 32, phase7, 0)
    pltpu.make_async_copy(recv4.at[parity], recv4.at[parity], r7).wait()
    cross7 = pltpu.make_async_remote_copy(
        src_ref=recv4.at[parity], dst_ref=recv4.at[parity], send_sem=s7c, recv_sem=r7c,
        device_id=twin, device_id_type=MESH,
    )
    cross7.start()
    pltpu.make_async_copy(recv4.at[other], recv4.at[other], r7c).wait()

    xbuf[...] = recv4[...].reshape(1024, 128).astype(F32)
    for t in range(2):
        for q in range(2):
            for pp in range(2):
                for hf in range(2):
                    for jb in range(3):
                        if jb == 0 and hf == 1:
                            continue
                        dst = 0 if jb == 0 else hf * 2 + jb
                        base = (pp * 32 + hf * 16) * 16 + (t * 2 + q) * 3 + jb
                        keyf[dst, pl.ds(t * GROUP + pp * 2 + q, 16, stride=4), :] = xbuf[
                            pl.ds(base, 16, stride=16), :
                        ]
    for b in range(4):
        glat_ref[:, b * 128:(b + 1) * 128] = keyf[b + 1].astype(BF16)
    grope_ref[...] = keyf[0][:, :ROPE].astype(BF16)

    def drain(ref, sem):
        pltpu.make_async_copy(ref, ref, sem).wait()

    drain(send1.at[pl.ds(0, 31)], s1)
    drain(send4.at[pl.ds(0, 31)], s7)
    cross1.wait_send()
    cross5.wait_send()
    cross6.wait_send()
    cross7.wait_send()

    @pl.when(core == 1)
    def _():
        drain(send1.at[0], s1x)
        drain(send4.at[0], s7x)

    for which in range(2):
        cross2[which].wait_send()
        drain(dsend.at[which], s3c.at[which])

        @pl.when(half == 0)
        def _():
            drain(send2.at[which, pl.ds(0, 31)], s2.at[which])

            @pl.when(core == 1)
            def _():
                drain(send2.at[which, 0], s2x.at[which])
                drain(recvb.at[which, 0], s4x.at[which])

        @pl.when(half == 1)
        def _():
            drain(send2.at[which, pl.ds(0, 31), :, pl.ds(128, 256)], s2.at[which])

            @pl.when(core == 1)
            def _():
                drain(send2.at[which, 0, :, pl.ds(128, 256)], s2x.at[which])
                drain(recvb.at[which, 0, :, pl.ds(128, 256)], s4x.at[which])

        @pl.when(half == 0)
        def _():
            drain(recvb.at[which, pl.ds(0, 15)], s4.at[which])
            drain(recvb.at[which, pl.ds(0, 16), :, pl.ds(128, 256)], s4.at[which])

        @pl.when(half == 1)
        def _():
            drain(recvb.at[which, pl.ds(0, 16)], s4.at[which])
            drain(recvb.at[which, pl.ds(0, 15), :, pl.ds(128, 256)], s4.at[which])

    for store in stores:
        store.wait()


def local(
    query_nope, query_rope, latent, key_rope, up_key, up_value, grad_out, group_order, tile_mask
):
    order_row = group_order.reshape(32, 2, 2).transpose(2, 1, 0).reshape(1, 128)
    vmem = pl.BlockSpec(memory_space=pltpu.VMEM)
    smem = pl.BlockSpec(memory_space=pltpu.SMEM)
    hbm = pl.BlockSpec(memory_space=pl.ANY)
    dma = pltpu.SemaphoreType.DMA
    scratch = [
        pltpu.VMEM((128, 2048), BF16),
        pltpu.VMEM((128, 1024), BF16),
        pltpu.VMEM((LATENT, 2048), BF16),
        pltpu.VMEM((LATENT, 2048), BF16),
        pltpu.VMEM((128, 2048), BF16),
        pltpu.VMEM((128, 2048), BF16),
        pltpu.VMEM((128, 2048), BF16),
        pltpu.VMEM((128, 1024), BF16),
        pltpu.VMEM((5, 128, 128), F32),
        pltpu.VMEM((1024, 128), F32),
        pltpu.VMEM((64, 16, 128), BF16),
        pltpu.VMEM((2, 32, 16, 128), BF16),
        pltpu.VMEM((256, 384), BF16),
        pltpu.VMEM((1024, 256), BF16),
        pltpu.VMEM((2, 32, 16, 384), BF16),
        pltpu.VMEM((2, 16, 2, 16, WIDTH), BF16),
        pltpu.VMEM((2, ROWS, WIDTH), BF16),
        pltpu.VMEM((2, ROWS, LATENT), BF16),
        pltpu.VMEM((HEAD_DEV, 128, LATENT), BF16),
        pltpu.VMEM((HEAD_DEV, 128, LATENT), BF16),
        pltpu.VMEM((ROWS, KEYS), BF16),
        pltpu.VMEM((ROWS, KEYS), BF16),
        pltpu.VMEM((2, GROUP, KEYS), F32),
        pltpu.VMEM((2, 16, 2, 16, WIDTH), F32),
        pltpu.VMEM((2, 16, 16, WIDTH), BF16),
        pltpu.VMEM((2, 16, 16, WIDTH), BF16),
        pltpu.VMEM((2, 16, 16, WIDTH), BF16),
        pltpu.VMEM((2, 32, 16, 384), BF16),
        pltpu.VMEM((4, 2, 32, 384), F32),
        pltpu.VMEM((4, 32, 384), F32),
        pltpu.VMEM((4, 32, 384), F32),
        pltpu.VMEM((4, 32, 384), F32),
        pltpu.VMEM((32, 16, 128), BF16),
        pltpu.VMEM((2, 32, 16, 128), BF16),
        dma((5,)), dma((3,)),
        dma, dma, dma, dma, dma,
        dma((2,)), dma((2,)), dma((2,)), dma((2,)), dma((2,)),
        dma((2,)), dma((2,)),
        dma((2,)), dma((2,)), dma((2,)),
        dma, dma, dma, dma,
        dma, dma, dma, dma, dma,
    ]
    return pl.pallas_call(
        kernel,
        out_shape=(
            jax.ShapeDtypeStruct((128, 2048), BF16),
            jax.ShapeDtypeStruct((128, 2048), BF16),
            jax.ShapeDtypeStruct((128, 1024), BF16),
            jax.ShapeDtypeStruct((128, LATENT), BF16),
            jax.ShapeDtypeStruct((128, ROPE), BF16),
        ),
        in_specs=[hbm, hbm, vmem, vmem, hbm, hbm, hbm, smem, vmem, vmem],
        out_specs=(hbm, hbm, hbm, vmem, vmem),
        scratch_shapes=scratch,
        compiler_params=pltpu.CompilerParams(
            collective_id=0, has_side_effects=True, vmem_limit_bytes=56 << 20
        ),
    )(
        query_nope, query_rope, latent, key_rope, up_key, up_value, grad_out,
        group_order, order_row, tile_mask,
    )


def solution(mesh):
    placed = (
        P("seq", "head"),
        P("seq", "head"),
        P("seq", None),
        P("seq", None),
        P(None, "head"),
        P(None, "head"),
        P("seq", "head"),
        P(),
        P(),
    )
    return jax.shard_map(
        local,
        mesh=mesh,
        in_specs=placed,
        out_specs=(
            P("seq", "head"),
            P("seq", "head"),
            P("seq", "head"),
            P("seq", None),
            P("seq", None),
        ),
        check_vma=False,
    )
```

time: 871 us -> 91.5 us (0.11)
  waiting for transfers between devices: 729 us -> 0 us
  Pallas kernels: 0 us -> 80.9 us
  other arithmetic: 33.2 us -> 0 us
  local copies, waits for them, and re-layouts: 41.6 us -> 9.56 us
  matrix products: 27.1 us -> 0 us
  blocking collectives: 19.8 us -> 0 us
  between operations: 19.9 us -> 0.67 us
    reduce_scatter x1 -> x0, waiting for transfers between devices: 480 us -> none  [local(): lax.psum_scatter(grad_flat, 'seq', scatter_dimension=0, tiled=True)]
    all_gather x1 -> x0, waiting for transfers between devices: 248 us -> none  [local(): key_rows = lax.all_gather(own_keys, 'seq', axis=0, tiled=True)]
    pallas_call x0 -> x1, Pallas kernels: none -> 80.9 us  [local(): pl.pallas_call(kernel, out_shape=(jax.ShapeDtypeStruct((128, 2048), BF16)...]
    dot_general x20 -> x0, matrix products: 27.1 us -> none  [the longest x4 6.53 us: window_product(): jnp.einsum('htc,kc->htk', left, right, preferred_element_type=jnp.float32)]
    psum x1 -> x0, blocking collectives: 19.8 us -> none  [local(): grad_keys = lax.psum(reduced, 'head').astype(jnp.bfloat16)]
    gather x5 -> x0, local copies, waits for them, and re-layouts: 12.1 us -> none  [the longest x2 10.1 us: local(): jnp.take(key_blocks, slots, axis=0).reshape(span * group_rows, width)]
    select_n x5 -> x0, other arithmetic: 12.1 us -> none  [the longest x1 10.2 us: local(): jnp.repeat(live, group_rows, total_repeat_length=span * group_rows)]
    broadcast_in_dim x2 -> x0, local copies, waits for them, and re-layouts: 10.5 us -> none  [the longest x1 9.6 us: local(): grad_full = jnp.zeros((group_count, group_rows, width), jnp.float32)]
  transfers between devices with their start and end apart: 2 -> 0, of which waited for: 2 -> 0; matrix products, arithmetic and copies ran while one was open for 5% -> 0% of each run, Pallas kernels for 0% -> 0%
where the time goes in v1:
time: 91.5 us; the launch traced here: 91.2 us
  Pallas kernels  80.9 us (88%)
  local copies, waits for them, and re-layouts  9.56 us (10%)
    pallas_call x1, Pallas kernels, local(): pl.pallas_call(kernel, out_shape=(jax.ShapeDtypeStruct((128, 2048), BF16)...  80.9 us
    unnamed x9, local copies, waits for them, and re-layouts  6.56 us

profile of v1, /device:TPU:1, one launch (start us, length us, event | category | flops | bytes accessed | tf_op | source)
XLA Modules:
  0.0 91.2 jit_solution(17777069282998535207)
XLA Ops:
  0.6 1.4 %copy.18.rope_ref = bf16[128,64]{1,0:T(8,128)(2,1)} copy(bf16[128,64]{0,1:T(8,128)(2,1)} %param.12) | data formatting | bytes 32768 | tf_op args[3]
  2.1 0.8 reshape.16
  2.9 0.1 copy.17
  3.0 0.6 reshape.17.order_row
  3.6 80.9 %shard_map.128 = (bf16[128,2048]{1,0:T(8,128)(2,1)}, bf16[128,2048]{1,0:T(8,128)(2,1)}, bf16[128,1024]{1,0:T(8,128)(2,1)}, bf16[128,512]{1,0:T(8,128)(2,1)}, bf16[128,64]{1,0:T(8,128)(2,1)}) custom-call(bf16[128,2048]{1,0:T(8,128)(2,1)} %qn_hbm.1, bf16[128,1024]{1,0:T(8,128)(2,1)} %qr_hbm.1, bf16[128,512]{1,0:T(8,128)(2,1)} %lat_ref.1, ...), custom_call_target="tpu_custom_call" | custom-call | tf_op jit(solution)/shard_map/pallas_call | solution.py:544
  84.5 0.0 copy-start
  84.5 0.0 copy-start.1
  84.6 1.5 %copy.19 = bf16[128,64]{0,1:T(8,128)(2,1)} copy(bf16[128,64]{1,0:T(8,128)(2,1)} %get-tuple-element.14) | data formatting | bytes 32768 | tf_op jit(solution)/shard_map/pallas_call | solution.py:544
  86.1 1.9 %copy.24 = bf16[128,2048]{1,0:T(8,128)(2,1)} copy(bf16[128,2048]{1,0:T(8,128)(2,1)} %get-tuple-element.20) | data formatting | bytes 1048576
  87.9 1.9 %copy.25 = bf16[128,2048]{1,0:T(8,128)(2,1)} copy(bf16[128,2048]{1,0:T(8,128)(2,1)} %get-tuple-element.21) | data formatting | bytes 1048576
  89.8 0.0 copy-done
  89.8 0.7 copy.26
  90.5 0.0 copy-done.1
  90.5 0.7 copy.27
Async XLA Ops:
  84.5 5.3 %copy-start = (bf16[128,1024]{1,0:T(8,128)(2,1)S(1)}, bf16[128,1024]{1,0:T(8,128)(2,1)}, u32[]{:S(2)}) copy-start(bf16[128,1024]{1,0:T(8,128)(2,1)} %get-tuple-element.22) | copy-start | bytes 786436
  84.5 6.0 %copy-start.1 = (bf16[128,512]{1,0:T(8,128)(2,1)S(1)}, bf16[128,512]{1,0:T(8,128)(2,1)}, u32[]{:S(2)}) copy-start(bf16[128,512]{1,0:T(8,128)(2,1)} %get-tuple-element.23) | copy-start | bytes 393220

commit v2 on v1

v2 whole, which is shorter than its diff:
```python
import functools
import math

import jax
import jax.numpy as jnp
from jax import lax
from jax.experimental import pallas as pl
from jax.experimental.pallas import tpu as pltpu
from jax.sharding import PartitionSpec as P

HEAD_DEV = 16
LATENT = 512
ROPE = 64
NOPE = 128
SPAN = 8
GROUP = 64
PAD = 128
WIDTH = PAD + LATENT
KEYS = SPAN * GROUP
ROWS = HEAD_DEV * GROUP
MESH = pl.DeviceIdType.MESH
SCALE = (NOPE + ROPE) ** (-0.5)
SCALE2 = SCALE * math.log2(math.e)
BLOCK = 256
F32 = jnp.float32
BF16 = jnp.bfloat16


def dot_nt(a, b):
    return lax.dot_general(a, b, (((1,), (1,)), ((), ())), preferred_element_type=F32)


def dot_nn(a, b):
    return lax.dot_general(a, b, (((1,), (0,)), ((), ())), preferred_element_type=F32)


def dot_tn(a, b):
    return lax.dot_general(a, b, (((0,), (0,)), ((), ())), preferred_element_type=F32)


def kernel(
    qn_hbm, qr_hbm, lat_ref, rope_ref, uk_hbm, uv_hbm, go_hbm, order_sm, order_ref, mask_hbm,
    out_hbm, gqn_hbm, gqr_hbm, glat_ref, grope_ref,
    qn, qr, uk, uv, gout, mask_ref, out_v, gqn_v, gqr_v,
    keyf, xbuf, send1, recv1, gather2, onehot, send2, window,
    qfull, glow, olat, gqlat, probs, dscore, bias,
    dwin, dsend, dpair, dmine, recvb, send7, recv7, part, fpart, home,
    insem, outsem, s1, r1, s2, r2, s2c, r2c,
    s3c, r3c, s4, r4, s7, r7, s8, r8, s9, r9,
):
    seq = lax.axis_index("seq")
    head = lax.axis_index("head")
    core = lax.rem(head, 2)
    x = lax.div(seq, 16)
    z = lax.rem(lax.div(seq, 2), 8)
    y = lax.rem(seq, 2)
    plane = lax.div(z, 4)
    piece = x * 8 + lax.rem(z, 4) * 2 + y
    twin = (seq, head + 1 - 2 * core)
    far = (seq, lax.rem(head + 2, 4))

    def around(i):
        return lax.rem(seq + i, 64)

    def piece_of(device):
        return lax.div(device, 16) * 8 + lax.rem(lax.div(device, 2), 4) * 2 + lax.rem(device, 2)

    def near(o, sign):
        step = lax.div(o, 8)
        shift = step + 5 * lax.div(step, 2) - 6 * lax.div(step, 3) + 4 * core * lax.div(step, 3)
        xo = lax.rem(lax.div(o, 2), 4)
        nx = lax.rem(x + 4 + sign * xo, 4)
        nz = lax.rem(z + 8 + sign * shift, 8)
        ny = lax.rem(y + lax.rem(o, 2), 2)
        return nx * 16 + nz * 2 + ny

    loads = [
        pltpu.make_async_copy(src, dst, insem.at[n])
        for n, (src, dst) in enumerate(
            [(qn_hbm, qn), (qr_hbm, qr), (uk_hbm, uk), (uv_hbm, uv), (go_hbm, gout), (mask_hbm, mask_ref)]
        )
    ]
    for load in loads:
        load.start()

    barrier = pltpu.get_barrier_semaphore()

    def greet(i, carry):
        pl.semaphore_signal(barrier, inc=1, device_id=(around(i), head), device_id_type=MESH)
        return carry

    lax.fori_loop(1, 64, greet, 0)
    pl.semaphore_signal(barrier, inc=1, device_id=twin, device_id_type=MESH)
    pl.semaphore_signal(barrier, inc=1, device_id=far, device_id_type=MESH)

    lanes = lax.broadcasted_iota(jnp.int32, (128, PAD), 1)
    rope = jnp.concatenate([rope_ref[...].astype(F32), jnp.zeros((PAD - ROPE, 128), F32)], 0)
    keyf[0] = rope.T
    for b in range(2):
        keyf[b + 1] = lat_ref[:, pl.ds(pl.multiple_of(core * 256 + b * 128, 128), 128)].astype(F32)
    xbuf[...] = jnp.zeros_like(xbuf)
    for t in range(2):
        for q in range(2):
            for jb in range(3):
                xbuf[pl.ds((t * 2 + q) * 3 + jb, 32, stride=16), :] = keyf[
                    jb, pl.ds(t * GROUP + q, 32, stride=2), :
                ]
    send1[...] = xbuf[pl.ds(0, 512), :].astype(BF16).reshape(32, 16, 128)

    sub = lax.broadcasted_iota(jnp.int32, (8, 128), 0)
    cin = lax.broadcasted_iota(jnp.int32, (128, 128), 0)
    cout = lax.broadcasted_iota(jnp.int32, (128, 128), 1)
    reorder = jnp.where(cin == 2 * lax.rem(cout, 64) + lax.div(cout, 64), 1.0, 0.0).astype(BF16)
    plain = jnp.broadcast_to(order_ref[...].astype(F32).reshape(1, 128), (8, 128)).astype(BF16)
    row = dot_nn(plain, reorder)
    zero8 = jnp.zeros((8, 128), F32)

    def fill(n, carry):
        which = lax.div(n, 32)
        group = order_sm[2 * near(lax.rem(n, 32), 1) + which]
        hot = jnp.where(row == (sub + (group - (SPAN - 1))).astype(F32), 1.0, 0.0).astype(F32)
        upper = jnp.concatenate([hot, zero8], 1)
        lower = jnp.concatenate([zero8, hot], 1)
        onehot[pl.ds(pl.multiple_of(n * 16, 16), 16), :] = jnp.concatenate([upper, lower], 0).astype(BF16)
        return carry

    lax.fori_loop(0, 64, fill, 0)
    recvb[...] = jnp.zeros_like(recvb)
    pl.semaphore_wait(barrier, 65)

    pltpu.make_async_copy(send1.at[piece], recv1.at[seq], r1).start()

    def phase1(i, carry):
        dst = around(i)
        pltpu.make_async_remote_copy(
            src_ref=send1.at[piece_of(dst)], dst_ref=recv1.at[seq], send_sem=s1, recv_sem=r1,
            device_id=(dst, head), device_id_type=MESH,
        ).start()
        return carry

    lax.fori_loop(1, 64, phase1, 0)

    for load in loads:
        load.wait()

    def project(h, carry):
        cols = pl.ds(pl.multiple_of(h * NOPE, NOPE), NOPE)
        rows = pl.ds(pl.multiple_of(h * GROUP, GROUP), GROUP)
        ql = dot_nt(qn[:, cols], uk[:, cols]).astype(BF16)
        gl = dot_nt(gout[:, cols], uv[:, cols]).astype(BF16)
        for w in range(2):
            qfull[w, rows, pl.ds(PAD, LATENT)] = ql[w * GROUP:(w + 1) * GROUP]
            glow[w, rows, :] = gl[w * GROUP:(w + 1) * GROUP]
        return carry

    lax.fori_loop(0, HEAD_DEV, project, 0)

    pltpu.make_async_copy(recv1, recv1, r1).wait()
    xbuf[...] = recv1[...].reshape(1024, 128).astype(F32)
    for q in range(2):
        for t in range(2):
            for jb in range(3):
                gather2[(q * 2 + t) * 64:(q * 2 + t + 1) * 64, jb * 128:(jb + 1) * 128] = xbuf[
                    pl.ds((t * 2 + q) * 3 + jb, 64, stride=16), :
                ].astype(BF16)

    def half_of(ref, cr):
        return ref if cr == 0 else ref.at[:, pl.ds(128, 256)]

    def columns(cr):
        return pl.ds(0, 384) if cr == 0 else pl.ds(384, 256)

    def by_core(run):
        for cr in range(2):
            @pl.when(core == cr)
            def _():
                run(cr)

    for which in range(2):
        picked = dot_nn(onehot[which * 512:(which + 1) * 512, :], gather2[...])
        send2[which] = picked.astype(BF16).reshape(32, 16, 384)

        def send_windows(cr):
            pltpu.make_async_copy(
                half_of(send2.at[which, 0], cr), window.at[which, piece, :, columns(cr)], r2.at[which]
            ).start()

            def phase2(o, carry):
                pltpu.make_async_remote_copy(
                    src_ref=half_of(send2.at[which, o], cr), dst_ref=window.at[which, piece, :, columns(cr)],
                    send_sem=s2.at[which], recv_sem=r2.at[which],
                    device_id=(near(o, 1), head), device_id_type=MESH,
                ).start()
                return carry

            lax.fori_loop(1, 32, phase2, 0)

        by_core(send_windows)

    def rotary(m, carry):
        two = qr[:, pl.ds(pl.multiple_of(m * 128, 128), 128)].astype(F32)
        even = jnp.where(lanes < ROPE, two, 0.0).astype(BF16)
        odd = jnp.where(lanes < ROPE, pltpu.roll(two, ROPE, 1), 0.0).astype(BF16)
        for w in range(2):
            qfull[w, pl.ds(pl.multiple_of(m * 128, 128), GROUP), pl.ds(0, PAD)] = even[w * GROUP:(w + 1) * GROUP]
            qfull[w, pl.ds(pl.multiple_of(m * 128 + GROUP, GROUP), GROUP), pl.ds(0, PAD)] = odd[
                w * GROUP:(w + 1) * GROUP
            ]
        return carry

    lax.fori_loop(0, HEAD_DEV // 2, rotary, 0)

    col = lax.broadcasted_iota(jnp.int32, (GROUP, KEYS), 1)
    slot = lax.rem(col, SPAN)
    key_row = lax.div(col, SPAN)
    query_row = lax.broadcasted_iota(jnp.int32, (GROUP, KEYS), 0)
    for which in range(2):
        group = order_sm[2 * seq + which]
        seen = jnp.sum(mask_ref[pl.ds(group, 1), :], axis=1, keepdims=True)
        allowed = (slot >= SPAN - seen) & ((slot < SPAN - 1) | (key_row <= query_row))
        bias[which] = jnp.where(allowed, 0.0, -1e30).astype(F32)

    def cross_copy(src, dst, sem_s, sem_r):
        return pltpu.make_async_remote_copy(
            src_ref=src, dst_ref=dst, send_sem=sem_s, recv_sem=sem_r, device_id=twin, device_id_type=MESH
        )

    def share_window(which):
        def run(cr):
            ref = window.at[which, :, :, columns(cr)]
            pltpu.make_async_copy(ref, ref, r2.at[which]).wait()
            cross_copy(ref, ref, s2c.at[which], r2c.at[which]).start()

        by_core(run)

    def await_window(which):
        def run(cr):
            ref = window.at[which, :, :, columns(1 - cr)]
            pltpu.make_async_copy(ref, ref, r2c.at[which]).wait()

        by_core(run)

    def attend_from(which, first, last):
        def attend(n, carry):
            rows = pl.ds(pl.multiple_of(n * BLOCK, BLOCK), BLOCK)
            keys = window[which].reshape(KEYS, WIDTH)
            lat = keys[:, PAD:]
            scores = dot_nt(qfull[which, rows, :], keys) * SCALE2
            scores = (scores.reshape(BLOCK // GROUP, GROUP, KEYS) + bias[which][None]).reshape(BLOCK, KEYS)
            top = jnp.max(scores, axis=1, keepdims=True)
            weights = jnp.exp2(scores - top)
            normed = weights * (1.0 / jnp.sum(weights, axis=1, keepdims=True))
            low = normed.astype(BF16)
            grad_prob = dot_nt(glow[which, rows, :], lat)
            prod = normed * grad_prob
            delta = jnp.sum(prod, axis=1, keepdims=True)
            ds = (prod - normed * delta).astype(BF16)
            probs[rows, :] = low
            dscore[rows, :] = ds
            ol = dot_nn(low, lat).astype(BF16)
            gq = (dot_nn(ds, keys) * SCALE).astype(BF16)
            for j in range(BLOCK // GROUP):
                part_rows = slice(j * GROUP, (j + 1) * GROUP)
                olat[n * (BLOCK // GROUP) + j, which * GROUP:(which + 1) * GROUP, :] = ol[part_rows]
                gqlat[n * (BLOCK // GROUP) + j, which * GROUP:(which + 1) * GROUP, :] = gq[part_rows, PAD:]
            for j in range(0, BLOCK // GROUP, 2):
                two = jnp.concatenate(
                    [gq[j * GROUP:(j + 1) * GROUP, :ROPE], gq[(j + 1) * GROUP:(j + 2) * GROUP, :ROPE]], 1
                )
                gqr_v[
                    which * GROUP:(which + 1) * GROUP, pl.ds(pl.multiple_of(n * BLOCK + j * ROPE, 128), 128)
                ] = two
            return carry

        lax.fori_loop(first, last, attend, 0)

    def key_grads(which):
        def key_grad(n, carry):
            krows = pl.ds(pl.multiple_of(n * 256, 256), 256)
            first = dot_tn(dscore[:, krows], qfull[which]) * SCALE
            second = dot_tn(probs[:, krows], glow[which])
            total = jnp.concatenate([first[:, :PAD], first[:, PAD:] + second], 1)
            dwin[which, pl.ds(n * 16, 16)] = total.reshape(16, 16, WIDTH)
            return carry

        lax.fori_loop(0, KEYS // 256, key_grad, 0)

    def share_grads(which):
        def run(cr):
            rest = columns(1 - cr)
            into = pl.ds(128, 256) if cr == 0 else pl.ds(0, 384)
            dsend[which, :, :, into] = dwin[which, :, :, rest].astype(BF16)
            cross_copy(
                dsend.at[which, :, :, into], dpair.at[which, :, :, into], s3c.at[which], r3c.at[which]
            ).start()

        by_core(run)

    def send_grads(which):
        def run(cr):
            into = pl.ds(0, 384) if cr == 0 else pl.ds(128, 256)
            ref = dpair.at[which, :, :, into]
            pltpu.make_async_copy(ref, ref, r3c.at[which]).wait()
            dmine[which, :, :, into] = (
                dwin[which, :, :, columns(cr)] + dpair[which, :, :, into].astype(F32)
            ).astype(BF16)
            pltpu.make_async_copy(
                half_of(dmine.at[which, piece], cr), half_of(recvb.at[which, 0], cr), r4.at[which]
            ).start()

            def phase4(o, carry):
                dst = near(o, -1)
                pltpu.make_async_remote_copy(
                    src_ref=half_of(dmine.at[which, piece_of(dst)], cr), dst_ref=half_of(recvb.at[which, o], cr),
                    send_sem=s4.at[which], recv_sem=r4.at[which], device_id=(dst, head), device_id_type=MESH,
                ).start()
                return carry

            lax.fori_loop(1, 32, phase4, 0)

        by_core(run)

    blocks = ROWS // BLOCK
    share_window(0)
    await_window(0)
    attend_from(0, 0, blocks)
    share_window(1)
    key_grads(0)
    share_grads(0)
    await_window(1)
    attend_from(1, 0, 1)
    send_grads(0)
    attend_from(1, 1, blocks)
    key_grads(1)
    share_grads(1)
    send_grads(1)

    def unproject(h, carry):
        cols = pl.ds(pl.multiple_of(h * NOPE, NOPE), NOPE)
        out_v[:, cols] = dot_nn(olat[h], uv[:, cols]).astype(BF16)
        gqn_v[:, cols] = dot_nn(gqlat[h], uk[:, cols]).astype(BF16)
        return carry

    lax.fori_loop(0, HEAD_DEV, unproject, 0)
    stores = [
        pltpu.make_async_copy(src, dst, outsem.at[n])
        for n, (src, dst) in enumerate([(out_v, out_hbm), (gqn_v, gqn_hbm), (gqr_v, gqr_hbm)])
    ]
    for store in stores:
        store.start()

    total = jnp.zeros((256, 384), F32)
    for which in range(2):
        def await_grads(cr):
            ref = recvb.at[which] if cr == 0 else recvb.at[which, :, :, pl.ds(128, 256)]
            pltpu.make_async_copy(ref, ref, r4.at[which]).wait()

        by_core(await_grads)
        total = total + dot_tn(onehot[which * 512:(which + 1) * 512, :], recvb[which].reshape(512, 384))
    for q in range(2):
        for t in range(2):
            for jb in range(3):
                xbuf[pl.ds((t * 2 + q) * 3 + jb, 64, stride=16), :] = total[
                    (q * 2 + t) * 64:(q * 2 + t + 1) * 64, jb * 128:(jb + 1) * 128
                ]
    send7[...] = xbuf[...].astype(BF16).reshape(64, 16, 128)

    pltpu.make_async_copy(send7.at[seq], recv7.at[plane, piece], r7).start()

    def phase7(i, carry):
        dst = around(i)
        pltpu.make_async_remote_copy(
            src_ref=send7.at[dst], dst_ref=recv7.at[plane, piece], send_sem=s7, recv_sem=r7,
            device_id=(dst, head), device_id_type=MESH,
        ).start()
        return carry

    lax.fori_loop(1, 64, phase7, 0)
    pltpu.make_async_copy(recv7, recv7, r7).wait()
    xbuf[pl.ds(0, 512), :] = (recv7[0].astype(F32) + recv7[1].astype(F32)).reshape(512, 128)
    for t in range(2):
        for q in range(2):
            for jb in range(3):
                keyf[jb, pl.ds(t * GROUP + q, 32, stride=2), :] = xbuf[
                    pl.ds((t * 2 + q) * 3 + jb, 32, stride=16), :
                ]
    part[...] = keyf[...].astype(BF16)

    def add_far(cr):
        blocks3 = pl.ds(0, 3) if cr == 0 else pl.ds(1, 2)
        mine = pl.ds(0, 3) if cr == 0 else pl.ds(3, 2)
        rest = pl.ds(3, 2) if cr == 0 else pl.ds(0, 3)
        copy = pltpu.make_async_remote_copy(
            src_ref=part.at[blocks3], dst_ref=fpart.at[blocks3], send_sem=s8, recv_sem=r8,
            device_id=far, device_id_type=MESH,
        )
        copy.start()
        copy.wait_recv()
        home[mine] = (part[blocks3].astype(F32) + fpart[blocks3].astype(F32)).astype(BF16)
        cross_copy(home.at[mine], home.at[mine], s9, r9).start()
        pltpu.make_async_copy(home.at[rest], home.at[rest], r9).wait()
        copy.wait_send()
        pltpu.make_async_copy(home.at[mine], home.at[mine], s9).wait()

    by_core(add_far)
    for b in range(4):
        glat_ref[:, b * 128:(b + 1) * 128] = home[b + 1]
    grope_ref[...] = home[0].astype(F32).T[:ROPE].astype(BF16)

    def drain(ref, sem):
        pltpu.make_async_copy(ref, ref, sem).wait()

    drain(recv1.at[pl.ds(0, 63)], s1)
    drain(send7.at[pl.ds(0, 63)], s7)

    def drain_halves(cr):
        for which in range(2):
            own = pl.ds(0, 384) if cr == 0 else pl.ds(128, 256)
            rest = pl.ds(128, 256) if cr == 0 else pl.ds(0, 384)
            drain(send2.at[which, pl.ds(0, 31), :, own], s2.at[which])
            drain(dmine.at[which, pl.ds(0, 31), :, own], s4.at[which])
            drain(window.at[which, :, :, columns(cr)], s2c.at[which])
            drain(dsend.at[which, :, :, rest], s3c.at[which])

    by_core(drain_halves)
    for store in stores:
        store.wait()


def copy_kernel(*refs):
    count = (len(refs) - 2) // 3
    srcs, dsts, held = refs[:count], refs[count:2 * count], refs[2 * count:3 * count]
    insem, outsem = refs[3 * count:]
    reads = [pltpu.make_async_copy(srcs[n], held[n], insem.at[n]) for n in range(count)]
    writes = [pltpu.make_async_copy(held[n], dsts[n], outsem.at[n]) for n in range(count)]
    for read in reads:
        read.start()
    for read, write in zip(reads, writes):
        read.wait()
        write.start()
    for write in writes:
        write.wait()


def local(
    query_nope, query_rope, latent, key_rope, up_key, up_value, grad_out, group_order, tile_mask
):
    vmem = pl.BlockSpec(memory_space=pltpu.VMEM)
    smem = pl.BlockSpec(memory_space=pltpu.SMEM)
    hbm = pl.BlockSpec(memory_space=pl.ANY)
    dma = pltpu.SemaphoreType.DMA
    scratch = [
        pltpu.VMEM((128, 2048), BF16),
        pltpu.VMEM((128, 1024), BF16),
        pltpu.VMEM((LATENT, 2048), BF16),
        pltpu.VMEM((LATENT, 2048), BF16),
        pltpu.VMEM((128, 2048), BF16),
        pltpu.VMEM((128, 128), jnp.int32),
        pltpu.VMEM((128, 2048), BF16),
        pltpu.VMEM((128, 2048), BF16),
        pltpu.VMEM((128, 1024), BF16),
        pltpu.VMEM((3, 128, 128), F32),
        pltpu.VMEM((1024, 128), F32),
        pltpu.VMEM((32, 16, 128), BF16),
        pltpu.VMEM((64, 16, 128), BF16),
        pltpu.VMEM((256, 384), BF16),
        pltpu.VMEM((1024, 256), BF16),
        pltpu.VMEM((2, 32, 16, 384), BF16),
        pltpu.VMEM((2, 32, 16, WIDTH), BF16),
        pltpu.VMEM((2, ROWS, WIDTH), BF16),
        pltpu.VMEM((2, ROWS, LATENT), BF16),
        pltpu.VMEM((HEAD_DEV, 128, LATENT), BF16),
        pltpu.VMEM((HEAD_DEV, 128, LATENT), BF16),
        pltpu.VMEM((ROWS, KEYS), BF16),
        pltpu.VMEM((ROWS, KEYS), BF16),
        pltpu.VMEM((2, GROUP, KEYS), F32),
        pltpu.VMEM((2, 32, 16, WIDTH), F32),
        pltpu.VMEM((2, 32, 16, 384), BF16),
        pltpu.VMEM((2, 32, 16, 384), BF16),
        pltpu.VMEM((2, 32, 16, 384), BF16),
        pltpu.VMEM((2, 32, 16, 384), BF16),
        pltpu.VMEM((64, 16, 128), BF16),
        pltpu.VMEM((2, 32, 16, 128), BF16),
        pltpu.VMEM((3, 128, 128), BF16),
        pltpu.VMEM((3, 128, 128), BF16),
        pltpu.VMEM((5, 128, 128), BF16),
        dma((6,)), dma((3,)),
        dma, dma,
        dma((2,)), dma((2,)), dma((2,)), dma((2,)),
        dma((2,)), dma((2,)),
        dma((2,)), dma((2,)),
        dma, dma, dma, dma, dma, dma,
    ]
    shapes = (
        jax.ShapeDtypeStruct((128, 2048), BF16),
        jax.ShapeDtypeStruct((128, 2048), BF16),
        jax.ShapeDtypeStruct((128, 1024), BF16),
        jax.ShapeDtypeStruct((128, LATENT), BF16),
        jax.ShapeDtypeStruct((ROPE, 128), BF16),
    )
    results = pl.pallas_call(
        kernel,
        out_shape=shapes,
        in_specs=[hbm, hbm, vmem, vmem, hbm, hbm, hbm, smem, vmem, hbm],
        out_specs=(hbm, hbm, hbm, vmem, vmem),
        scratch_shapes=scratch,
        compiler_params=pltpu.CompilerParams(
            collective_id=0, has_side_effects=True, vmem_limit_bytes=56 << 20
        ),
    )(
        query_nope, query_rope, latent, key_rope.T, up_key, up_value, grad_out,
        group_order, group_order, tile_mask,
    )
    out, gqn, gqr, glat, grope = pl.pallas_call(
        copy_kernel,
        out_shape=shapes,
        in_specs=[hbm] * 5,
        out_specs=(hbm,) * 5,
        scratch_shapes=[pltpu.VMEM(a.shape, a.dtype) for a in shapes] + [dma((5,)), dma((5,))],
    )(*results)
    return out, gqn, gqr, glat, grope.T


def solution(mesh):
    placed = (
        P("seq", "head"),
        P("seq", "head"),
        P("seq", None),
        P("seq", None),
        P(None, "head"),
        P(None, "head"),
        P("seq", "head"),
        P(),
        P(),
    )
    return jax.shard_map(
        local,
        mesh=mesh,
        in_specs=placed,
        out_specs=(
            P("seq", "head"),
            P("seq", "head"),
            P("seq", "head"),
            P("seq", None),
            P("seq", None),
        ),
        check_vma=False,
    )
```

time: 91.5 us -> 75.5 us (0.83)
  local copies, waits for them, and re-layouts: 9.56 us -> 0 us
  Pallas kernels: 80.9 us -> 74.8 us
    unnamed x9 -> x0, local copies, waits for them, and re-layouts: 6.56 us -> none
    pallas_call x1 -> x2, Pallas kernels: 80.9 us -> 74.8 us  [the longest x1 72.6 us: local(): pl.pallas_call(kernel, out_shape=shapes, in_specs=[hbm, hbm, vmem, vmem,...]
    pallas_call x1 -> x0, local copies, waits for them, and re-layouts: 1.5 us -> none  [local(): pl.pallas_call(kernel, out_shape=(jax.ShapeDtypeStruct((128, 2048), BF16)...]
    reshape x2 -> x0, local copies, waits for them, and re-layouts: 1.42 us -> none  [local(): order_row = group_order.reshape(32, 2, 2).transpose(2, 1, 0).reshape(1, 128)]
where the time goes in v2:
time: 75.5 us; the launch traced here: 75.4 us
  Pallas kernels  74.8 us (99%)
    pallas_call x1, Pallas kernels, local(): pl.pallas_call(kernel, out_shape=shapes, in_specs=[hbm, hbm, vmem, vmem,...  72.6 us
    pallas_call x1, Pallas kernels, local(): pl.pallas_call(copy_kernel, out_shape=shapes, in_specs=[hbm] * 5, out_spe...  2.22 us

profile of v2, /device:TPU:1, one launch (start us, length us, event | category | flops | bytes accessed | tf_op | source)
XLA Modules:
  0.0 75.4 jit_solution(15649955775034598338)
XLA Ops:
  0.6 72.6 %shard_map.128 = (bf16[128,2048]{1,0:T(8,128)(2,1)}, bf16[128,2048]{1,0:T(8,128)(2,1)}, bf16[128,1024]{1,0:T(8,128)(2,1)}, bf16[128,512]{1,0:T(8,128)(2,1)}, bf16[64,128]{1,0:T(8,128)(2,1)}) custom-call(bf16[128,2048]{1,0:T(8,128)(2,1)} %qn_hbm.1, bf16[128,1024]{1,0:T(8,128)(2,1)} %qr_hbm.1, bf16[128,512]{1,0:T(8,128)(2,1)} %lat_ref.1, ...), custom_call_target="tpu_custom_call" | custom-call | tf_op jit(solution)/shard_map/pallas_call | solution.py:501
  73.2 2.2 %shard_map.129 = (bf16[128,2048]{1,0:T(8,128)(2,1)}, bf16[128,2048]{1,0:T(8,128)(2,1)}, bf16[128,1024]{1,0:T(8,128)(2,1)}, bf16[128,512]{1,0:T(8,128)(2,1)}, bf16[64,128]{1,0:T(8,128)(2,1)}) custom-call(bf16[128,2048]{1,0:T(8,128)(2,1)} %get-tuple-element.15.refs_0_, bf16[128,2048]{1,0:T(8,128)(2,1)} %get-tuple-element.16.refs_1_, ...), custom_call_target="tpu_custom_call" | custom-call | tf_op jit(solution)/shard_map/pallas_call | solution.py:514

commit v3 on v2

--- a/solution.py
+++ b/solution.py
@@ -21,7 +21,8 @@
 MESH = pl.DeviceIdType.MESH
 SCALE = (NOPE + ROPE) ** (-0.5)
 SCALE2 = SCALE * math.log2(math.e)
-BLOCK = 256
+BLOCK = 512
+SUB = 256
 F32 = jnp.float32
 BF16 = jnp.bfloat16
 
@@ -44,7 +45,7 @@
     qn, qr, uk, uv, gout, mask_ref, out_v, gqn_v, gqr_v,
     keyf, xbuf, send1, recv1, gather2, onehot, send2, window,
     qfull, glow, olat, gqlat, probs, dscore, bias,
-    dwin, dsend, dpair, dmine, recvb, send7, recv7, part, fpart, home,
+    dwin, dsend, dpair, dmine, recvb, onehot_t, send7, recv7, part, fpart, home,
     insem, outsem, s1, r1, s2, r2, s2c, r2c,
     s3c, r3c, s4, r4, s7, r7, s8, r8, s9, r9,
 ):
@@ -225,6 +226,9 @@
             src_ref=src, dst_ref=dst, send_sem=sem_s, recv_sem=sem_r, device_id=twin, device_id_type=MESH
         )
 
+    for which in range(2):
+        onehot_t[which] = onehot[which * 512:(which + 1) * 512, :].T
+
     def share_window(which):
         def run(cr):
             ref = window.at[which, :, :, columns(cr)]
@@ -242,34 +246,38 @@
 
     def attend_from(which, first, last):
         def attend(n, carry):
-            rows = pl.ds(pl.multiple_of(n * BLOCK, BLOCK), BLOCK)
             keys = window[which].reshape(KEYS, WIDTH)
             lat = keys[:, PAD:]
-            scores = dot_nt(qfull[which, rows, :], keys) * SCALE2
-            scores = (scores.reshape(BLOCK // GROUP, GROUP, KEYS) + bias[which][None]).reshape(BLOCK, KEYS)
-            top = jnp.max(scores, axis=1, keepdims=True)
-            weights = jnp.exp2(scores - top)
-            normed = weights * (1.0 / jnp.sum(weights, axis=1, keepdims=True))
-            low = normed.astype(BF16)
-            grad_prob = dot_nt(glow[which, rows, :], lat)
-            prod = normed * grad_prob
-            delta = jnp.sum(prod, axis=1, keepdims=True)
-            ds = (prod - normed * delta).astype(BF16)
-            probs[rows, :] = low
-            dscore[rows, :] = ds
-            ol = dot_nn(low, lat).astype(BF16)
-            gq = (dot_nn(ds, keys) * SCALE).astype(BF16)
-            for j in range(BLOCK // GROUP):
-                part_rows = slice(j * GROUP, (j + 1) * GROUP)
-                olat[n * (BLOCK // GROUP) + j, which * GROUP:(which + 1) * GROUP, :] = ol[part_rows]
-                gqlat[n * (BLOCK // GROUP) + j, which * GROUP:(which + 1) * GROUP, :] = gq[part_rows, PAD:]
-            for j in range(0, BLOCK // GROUP, 2):
-                two = jnp.concatenate(
-                    [gq[j * GROUP:(j + 1) * GROUP, :ROPE], gq[(j + 1) * GROUP:(j + 2) * GROUP, :ROPE]], 1
-                )
-                gqr_v[
-                    which * GROUP:(which + 1) * GROUP, pl.ds(pl.multiple_of(n * BLOCK + j * ROPE, 128), 128)
-                ] = two
+            parts = [pl.ds(pl.multiple_of(n * BLOCK + i * SUB, SUB), SUB) for i in range(BLOCK // SUB)]
+            scores = [dot_nt(qfull[which, rows, :], keys) for rows in parts]
+            grad_prob = [dot_nt(glow[which, rows, :], lat) for rows in parts]
+            for i, rows in enumerate(parts):
+                score = scores[i] * SCALE2
+                score = (score.reshape(SUB // GROUP, GROUP, KEYS) + bias[which][None]).reshape(SUB, KEYS)
+                top = jnp.max(score, axis=1, keepdims=True)
+                weights = jnp.exp2(score - top)
+                normed = weights * (1.0 / jnp.sum(weights, axis=1, keepdims=True))
+                low = normed.astype(BF16)
+                probs[rows, :] = low
+                ol = dot_nn(low, lat).astype(BF16)
+                prod = normed * grad_prob[i]
+                delta = jnp.sum(prod, axis=1, keepdims=True)
+                ds = (prod - normed * delta).astype(BF16)
+                dscore[rows, :] = ds
+                gq = (dot_nn(ds, keys) * SCALE).astype(BF16)
+                first_head = n * (BLOCK // GROUP) + i * (SUB // GROUP)
+                for j in range(SUB // GROUP):
+                    part_rows = slice(j * GROUP, (j + 1) * GROUP)
+                    olat[first_head + j, which * GROUP:(which + 1) * GROUP, :] = ol[part_rows]
+                    gqlat[first_head + j, which * GROUP:(which + 1) * GROUP, :] = gq[part_rows, PAD:]
+                for j in range(0, SUB // GROUP, 2):
+                    two = jnp.concatenate(
+                        [gq[j * GROUP:(j + 1) * GROUP, :ROPE], gq[(j + 1) * GROUP:(j + 2) * GROUP, :ROPE]], 1
+                    )
+                    gqr_v[
+                        which * GROUP:(which + 1) * GROUP,
+                        pl.ds(pl.multiple_of(n * BLOCK + i * SUB + j * ROPE, 128), 128),
+                    ] = two
             return carry
 
         lax.fori_loop(first, last, attend, 0)
@@ -308,7 +316,8 @@
                 half_of(dmine.at[which, piece], cr), half_of(recvb.at[which, 0], cr), r4.at[which]
             ).start()
 
-            def phase4(o, carry):
+            def phase4(i, carry):
+                o = 32 - i
                 dst = near(o, -1)
                 pltpu.make_async_remote_copy(
                     src_ref=half_of(dmine.at[which, piece_of(dst)], cr), dst_ref=half_of(recvb.at[which, o], cr),
@@ -356,7 +365,7 @@
             pltpu.make_async_copy(ref, ref, r4.at[which]).wait()
 
         by_core(await_grads)
-        total = total + dot_tn(onehot[which * 512:(which + 1) * 512, :], recvb[which].reshape(512, 384))
+        total = total + dot_nn(onehot_t[which], recvb[which].reshape(512, 384))
     for q in range(2):
         for t in range(2):
             for jb in range(3):
@@ -479,6 +488,7 @@
         pltpu.VMEM((2, 32, 16, 384), BF16),
         pltpu.VMEM((2, 32, 16, 384), BF16),
         pltpu.VMEM((2, 32, 16, 384), BF16),
+        pltpu.VMEM((2, 256, 512), BF16),
         pltpu.VMEM((64, 16, 128), BF16),
         pltpu.VMEM((2, 32, 16, 128), BF16),
         pltpu.VMEM((3, 128, 128), BF16),

time: 75.5 us -> 71.8 us (0.951)
  Pallas kernels: 74.8 us -> 71.1 us
    pallas_call x1, Pallas kernels: 72.6 us -> 68.8 us  [local(): pl.pallas_call(kernel, out_shape=shapes, in_specs=[hbm, hbm, vmem, vmem,...]
where the time goes in v3:
time: 71.8 us; the launch traced here: 71.7 us
  Pallas kernels  71.1 us (99%)
    pallas_call x1, Pallas kernels, local(): pl.pallas_call(kernel, out_shape=shapes, in_specs=[hbm, hbm, vmem, vmem,...  68.8 us
    pallas_call x1, Pallas kernels, local(): pl.pallas_call(copy_kernel, out_shape=shapes, in_specs=[hbm] * 5, out_spe...  2.22 us

profile of v3, /device:TPU:1, one launch (start us, length us, event | category | flops | bytes accessed | tf_op | source)
XLA Modules:
  0.0 71.7 jit_solution(6085078010027645928)
XLA Ops:
  0.6 68.8 %shard_map.128 = (bf16[128,2048]{1,0:T(8,128)(2,1)}, bf16[128,2048]{1,0:T(8,128)(2,1)}, bf16[128,1024]{1,0:T(8,128)(2,1)}, bf16[128,512]{1,0:T(8,128)(2,1)}, bf16[64,128]{1,0:T(8,128)(2,1)}) custom-call(bf16[128,2048]{1,0:T(8,128)(2,1)} %qn_hbm.1, bf16[128,1024]{1,0:T(8,128)(2,1)} %qr_hbm.1, bf16[128,512]{1,0:T(8,128)(2,1)} %lat_ref.1, ...), custom_call_target="tpu_custom_call" | custom-call | tf_op jit(solution)/shard_map/pallas_call | solution.py:511
  69.5 2.2 %shard_map.129 = (bf16[128,2048]{1,0:T(8,128)(2,1)}, bf16[128,2048]{1,0:T(8,128)(2,1)}, bf16[128,1024]{1,0:T(8,128)(2,1)}, bf16[128,512]{1,0:T(8,128)(2,1)}, bf16[64,128]{1,0:T(8,128)(2,1)}) custom-call(bf16[128,2048]{1,0:T(8,128)(2,1)} %get-tuple-element.15.refs_0_, bf16[128,2048]{1,0:T(8,128)(2,1)} %get-tuple-element.16.refs_1_, ...), custom_call_target="tpu_custom_call" | custom-call | tf_op jit(solution)/shard_map/pallas_call | solution.py:524

commit v4 on v3

--- a/solution.py
+++ b/solution.py
@@ -40,14 +40,14 @@
 
 
 def kernel(
-    qn_hbm, qr_hbm, lat_ref, rope_ref, uk_hbm, uv_hbm, go_hbm, order_sm, order_ref, mask_hbm,
+    qn_hbm, qr_hbm, lat_hbm, rope_hbm, uk_hbm, uv_hbm, go_hbm, order_hbm, mask_hbm,
     out_hbm, gqn_hbm, gqr_hbm, glat_ref, grope_ref,
-    qn, qr, uk, uv, gout, mask_ref, out_v, gqn_v, gqr_v,
+    lat_ref, rope_ref, order_sm, order_ref, qn, qr, uk, uv, gout, mask_ref, out_v, gqn_v, gqr_v,
     keyf, xbuf, send1, recv1, gather2, onehot, send2, window,
     qfull, glow, olat, gqlat, probs, dscore, bias,
-    dwin, dsend, dpair, dmine, recvb, onehot_t, send7, recv7, part, fpart, home,
+    dwin, dsend, dpair, dmine, recvb, onehot_t, send7, recv7, home,
     insem, outsem, s1, r1, s2, r2, s2c, r2c,
-    s3c, r3c, s4, r4, s7, r7, s8, r8, s9, r9,
+    s3c, r3c, s4, r4, s7, r7, s9, r9,
 ):
     seq = lax.axis_index("seq")
     head = lax.axis_index("head")
@@ -59,6 +59,7 @@
     piece = x * 8 + lax.rem(z, 4) * 2 + y
     twin = (seq, head + 1 - 2 * core)
     far = (seq, lax.rem(head + 2, 4))
+    far_twin = (seq, lax.rem(head + 3 - 2 * core, 4))
 
     def around(i):
         return lax.rem(seq + i, 64)
@@ -75,8 +76,27 @@
         ny = lax.rem(y + lax.rem(o, 2), 2)
         return nx * 16 + nz * 2 + ny
 
+    barrier = pltpu.get_barrier_semaphore()
+
+    def greet(i, carry):
+        pl.semaphore_signal(barrier, inc=1, device_id=(around(i), head), device_id_type=MESH)
+        return carry
+
+    lax.fori_loop(1, 64, greet, 0)
+    pl.semaphore_signal(barrier, inc=1, device_id=twin, device_id_type=MESH)
+    pl.semaphore_signal(barrier, inc=1, device_id=far, device_id_type=MESH)
+    pl.semaphore_signal(barrier, inc=1, device_id=far_twin, device_id_type=MESH)
+
+    early = [
+        pltpu.make_async_copy(src, dst, insem.at[n])
+        for n, (src, dst) in enumerate(
+            [(lat_hbm, lat_ref), (rope_hbm, rope_ref), (order_hbm, order_ref), (order_hbm, order_sm)]
+        )
+    ]
+    for load in early:
+        load.start()
     loads = [
-        pltpu.make_async_copy(src, dst, insem.at[n])
+        pltpu.make_async_copy(src, dst, insem.at[4 + n])
         for n, (src, dst) in enumerate(
             [(qn_hbm, qn), (qr_hbm, qr), (uk_hbm, uk), (uv_hbm, uv), (go_hbm, gout), (mask_hbm, mask_ref)]
         )
@@ -84,15 +104,8 @@
     for load in loads:
         load.start()
 
-    barrier = pltpu.get_barrier_semaphore()
-
-    def greet(i, carry):
-        pl.semaphore_signal(barrier, inc=1, device_id=(around(i), head), device_id_type=MESH)
-        return carry
-
-    lax.fori_loop(1, 64, greet, 0)
-    pl.semaphore_signal(barrier, inc=1, device_id=twin, device_id_type=MESH)
-    pl.semaphore_signal(barrier, inc=1, device_id=far, device_id_type=MESH)
+    for load in early:
+        load.wait()
 
     lanes = lax.broadcasted_iota(jnp.int32, (128, PAD), 1)
     rope = jnp.concatenate([rope_ref[...].astype(F32), jnp.zeros((PAD - ROPE, 128), F32)], 0)
@@ -127,7 +140,7 @@
 
     lax.fori_loop(0, 64, fill, 0)
     recvb[...] = jnp.zeros_like(recvb)
-    pl.semaphore_wait(barrier, 65)
+    pl.semaphore_wait(barrier, 66)
 
     pltpu.make_async_copy(send1.at[piece], recv1.at[seq], r1).start()
 
@@ -282,50 +295,59 @@
 
         lax.fori_loop(first, last, attend, 0)
 
-    def key_grads(which):
-        def key_grad(n, carry):
-            krows = pl.ds(pl.multiple_of(n * 256, 256), 256)
-            first = dot_tn(dscore[:, krows], qfull[which]) * SCALE
-            second = dot_tn(probs[:, krows], glow[which])
-            total = jnp.concatenate([first[:, :PAD], first[:, PAD:] + second], 1)
-            dwin[which, pl.ds(n * 16, 16)] = total.reshape(16, 16, WIDTH)
-            return carry
-
-        lax.fori_loop(0, KEYS // 256, key_grad, 0)
-
-    def share_grads(which):
+    def key_grads(which, h):
+        krows = slice(h * 256, (h + 1) * 256)
+        first = dot_tn(dscore[:, krows], qfull[which]) * SCALE
+        second = dot_tn(probs[:, krows], glow[which])
+        total = jnp.concatenate([first[:, :PAD], first[:, PAD:] + second], 1)
+        dwin[which, h * 16:(h + 1) * 16] = total.reshape(16, 16, WIDTH)
+
+    def share_grads(which, h):
+        some = pl.ds(h * 16, 16)
+
         def run(cr):
             rest = columns(1 - cr)
             into = pl.ds(128, 256) if cr == 0 else pl.ds(0, 384)
-            dsend[which, :, :, into] = dwin[which, :, :, rest].astype(BF16)
+            dsend[which, some, :, into] = dwin[which, some, :, rest].astype(BF16)
             cross_copy(
-                dsend.at[which, :, :, into], dpair.at[which, :, :, into], s3c.at[which], r3c.at[which]
+                dsend.at[which, some, :, into], dpair.at[which, some, :, into],
+                s3c.at[2 * which + h], r3c.at[2 * which + h],
             ).start()
 
         by_core(run)
 
-    def send_grads(which):
+    def send_grads(which, h):
+        some = pl.ds(h * 16, 16)
+
         def run(cr):
             into = pl.ds(0, 384) if cr == 0 else pl.ds(128, 256)
-            ref = dpair.at[which, :, :, into]
-            pltpu.make_async_copy(ref, ref, r3c.at[which]).wait()
-            dmine[which, :, :, into] = (
-                dwin[which, :, :, columns(cr)] + dpair[which, :, :, into].astype(F32)
+            ref = dpair.at[which, some, :, into]
+            pltpu.make_async_copy(ref, ref, r3c.at[2 * which + h]).wait()
+            dmine[which, some, :, into] = (
+                dwin[which, some, :, columns(cr)] + dpair[which, some, :, into].astype(F32)
             ).astype(BF16)
-            pltpu.make_async_copy(
-                half_of(dmine.at[which, piece], cr), half_of(recvb.at[which, 0], cr), r4.at[which]
-            ).start()
 
             def phase4(i, carry):
-                o = 32 - i
+                xo = lax.rem(x + 4 - (2 * h + lax.rem(lax.div(i, 2), 2)), 4)
+                o = (3 - lax.div(i, 4)) * 8 + xo * 2 + lax.rem(i, 2)
                 dst = near(o, -1)
-                pltpu.make_async_remote_copy(
-                    src_ref=half_of(dmine.at[which, piece_of(dst)], cr), dst_ref=half_of(recvb.at[which, o], cr),
-                    send_sem=s4.at[which], recv_sem=r4.at[which], device_id=(dst, head), device_id_type=MESH,
-                ).start()
+                src_ref = half_of(dmine.at[which, piece_of(dst)], cr)
+                dst_ref = half_of(recvb.at[which, o], cr)
+
+                @pl.when(o == 0)
+                def _():
+                    pltpu.make_async_copy(src_ref, dst_ref, r4.at[which]).start()
+
+                @pl.when(o != 0)
+                def _():
+                    pltpu.make_async_remote_copy(
+                        src_ref=src_ref, dst_ref=dst_ref, send_sem=s4.at[which], recv_sem=r4.at[which],
+                        device_id=(dst, head), device_id_type=MESH,
+                    ).start()
+
                 return carry
 
-            lax.fori_loop(1, 32, phase4, 0)
+            lax.fori_loop(0, 16, phase4, 0)
 
         by_core(run)
 
@@ -334,15 +356,19 @@
     await_window(0)
     attend_from(0, 0, blocks)
     share_window(1)
-    key_grads(0)
-    share_grads(0)
+    for h in range(2):
+        key_grads(0, h)
+        share_grads(0, h)
     await_window(1)
     attend_from(1, 0, 1)
-    send_grads(0)
+    for h in range(2):
+        send_grads(0, h)
     attend_from(1, 1, blocks)
-    key_grads(1)
-    share_grads(1)
-    send_grads(1)
+    for h in range(2):
+        key_grads(1, h)
+        share_grads(1, h)
+    for h in range(2):
+        send_grads(1, h)
 
     def unproject(h, carry):
         cols = pl.ds(pl.multiple_of(h * NOPE, NOPE), NOPE)
@@ -393,28 +419,25 @@
                 keyf[jb, pl.ds(t * GROUP + q, 32, stride=2), :] = xbuf[
                     pl.ds((t * 2 + q) * 3 + jb, 32, stride=16), :
                 ]
-    part[...] = keyf[...].astype(BF16)
-
-    def add_far(cr):
-        blocks3 = pl.ds(0, 3) if cr == 0 else pl.ds(1, 2)
-        mine = pl.ds(0, 3) if cr == 0 else pl.ds(3, 2)
-        rest = pl.ds(3, 2) if cr == 0 else pl.ds(0, 3)
-        copy = pltpu.make_async_remote_copy(
-            src_ref=part.at[blocks3], dst_ref=fpart.at[blocks3], send_sem=s8, recv_sem=r8,
-            device_id=far, device_id_type=MESH,
-        )
-        copy.start()
-        copy.wait_recv()
-        home[mine] = (part[blocks3].astype(F32) + fpart[blocks3].astype(F32)).astype(BF16)
-        cross_copy(home.at[mine], home.at[mine], s9, r9).start()
-        pltpu.make_async_copy(home.at[rest], home.at[rest], r9).wait()
-        copy.wait_send()
-        pltpu.make_async_copy(home.at[mine], home.at[mine], s9).wait()
-
-    by_core(add_far)
+    home[pl.ds(head * 3, 3)] = keyf[...].astype(BF16)
+
+    def send_home(cr):
+        ref = home.at[pl.ds(head * 3 + cr, 3 - cr)]
+        for dst in (far, far_twin, twin):
+            pltpu.make_async_remote_copy(
+                src_ref=ref, dst_ref=ref, send_sem=s9, recv_sem=r9, device_id=dst, device_id_type=MESH
+            ).start()
+        got = home.at[pl.ds(0, 7 + cr)]
+        pltpu.make_async_copy(got, got, r9).wait()
+
+    by_core(send_home)
+
+    def both(block):
+        return home[block].astype(F32) + home[block + 6].astype(F32)
+
     for b in range(4):
-        glat_ref[:, b * 128:(b + 1) * 128] = home[b + 1]
-    grope_ref[...] = home[0].astype(F32).T[:ROPE].astype(BF16)
+        glat_ref[:, b * 128:(b + 1) * 128] = both(b // 2 * 3 + b % 2 + 1).astype(BF16)
+    grope_ref[...] = both(0).T[:ROPE].astype(BF16)
 
     def drain(ref, sem):
         pltpu.make_async_copy(ref, ref, sem).wait()
@@ -429,9 +452,16 @@
             drain(send2.at[which, pl.ds(0, 31), :, own], s2.at[which])
             drain(dmine.at[which, pl.ds(0, 31), :, own], s4.at[which])
             drain(window.at[which, :, :, columns(cr)], s2c.at[which])
-            drain(dsend.at[which, :, :, rest], s3c.at[which])
+            for h in range(2):
+                drain(dsend.at[which, pl.ds(h * 16, 16), :, rest], s3c.at[2 * which + h])
 
     by_core(drain_halves)
+
+    def drain_home(cr):
+        ref = home.at[pl.ds(0, 3 * (3 - cr))]
+        drain(ref, s9)
+
+    by_core(drain_home)
     for store in stores:
         store.wait()
 
@@ -455,10 +485,13 @@
     query_nope, query_rope, latent, key_rope, up_key, up_value, grad_out, group_order, tile_mask
 ):
     vmem = pl.BlockSpec(memory_space=pltpu.VMEM)
-    smem = pl.BlockSpec(memory_space=pltpu.SMEM)
     hbm = pl.BlockSpec(memory_space=pl.ANY)
     dma = pltpu.SemaphoreType.DMA
     scratch = [
+        pltpu.VMEM((128, LATENT), BF16),
+        pltpu.VMEM((ROPE, 128), BF16),
+        pltpu.SMEM((128,), jnp.int32),
+        pltpu.VMEM((128,), jnp.int32),
         pltpu.VMEM((128, 2048), BF16),
         pltpu.VMEM((128, 1024), BF16),
         pltpu.VMEM((LATENT, 2048), BF16),
@@ -491,15 +524,13 @@
         pltpu.VMEM((2, 256, 512), BF16),
         pltpu.VMEM((64, 16, 128), BF16),
         pltpu.VMEM((2, 32, 16, 128), BF16),
-        pltpu.VMEM((3, 128, 128), BF16),
-        pltpu.VMEM((3, 128, 128), BF16),
-        pltpu.VMEM((5, 128, 128), BF16),
-        dma((6,)), dma((3,)),
+        pltpu.VMEM((12, 128, 128), BF16),
+        dma((10,)), dma((3,)),
         dma, dma,
         dma((2,)), dma((2,)), dma((2,)), dma((2,)),
+        dma((4,)), dma((4,)),
         dma((2,)), dma((2,)),
-        dma((2,)), dma((2,)),
-        dma, dma, dma, dma, dma, dma,
+        dma, dma, dma, dma,
     ]
     shapes = (
         jax.ShapeDtypeStruct((128, 2048), BF16),
@@ -511,7 +542,7 @@
     results = pl.pallas_call(
         kernel,
         out_shape=shapes,
-        in_specs=[hbm, hbm, vmem, vmem, hbm, hbm, hbm, smem, vmem, hbm],
+        in_specs=[hbm] * 9,
         out_specs=(hbm, hbm, hbm, vmem, vmem),
         scratch_shapes=scratch,
         compiler_params=pltpu.CompilerParams(
@@ -519,7 +550,7 @@
         ),
     )(
         query_nope, query_rope, latent, key_rope.T, up_key, up_value, grad_out,
-        group_order, group_order, tile_mask,
+        group_order, tile_mask,
     )
     out, gqn, gqr, glat, grope = pl.pallas_call(
         copy_kernel,

time: 71.8 us -> 70.2 us (0.978)
  Pallas kernels: 71.1 us -> 69.4 us
    pallas_call x1, Pallas kernels: 68.8 us -> 67.2 us  [local(): pl.pallas_call(kernel, out_shape=shapes, in_specs=[hbm] * 9, out_specs=(h...]
where the time goes in v4:
time: 70.2 us; the launch traced here: 70.1 us
  Pallas kernels  69.4 us (99%)
    pallas_call x1, Pallas kernels, local(): pl.pallas_call(kernel, out_shape=shapes, in_specs=[hbm] * 9, out_specs=(h...  67.2 us
    pallas_call x1, Pallas kernels, local(): pl.pallas_call(copy_kernel, out_shape=shapes, in_specs=[hbm] * 5, out_spe...  2.22 us

profile of v4, /device:TPU:1, one launch (start us, length us, event | category | flops | bytes accessed | tf_op | source)
XLA Modules:
  0.0 70.1 jit_solution(6230449187006551759)
XLA Ops:
  0.6 67.2 %shard_map.128 = (bf16[128,2048]{1,0:T(8,128)(2,1)}, bf16[128,2048]{1,0:T(8,128)(2,1)}, bf16[128,1024]{1,0:T(8,128)(2,1)}, bf16[128,512]{1,0:T(8,128)(2,1)}, bf16[64,128]{1,0:T(8,128)(2,1)}) custom-call(bf16[128,2048]{1,0:T(8,128)(2,1)} %qn_hbm.1, bf16[128,1024]{1,0:T(8,128)(2,1)} %qr_hbm.1, bf16[128,512]{1,0:T(8,128)(2,1)} %lat_hbm.1, ...), custom_call_target="tpu_custom_call" | custom-call | tf_op jit(solution)/shard_map/pallas_call | solution.py:542
  67.9 2.2 %shard_map.129 = (bf16[128,2048]{1,0:T(8,128)(2,1)}, bf16[128,2048]{1,0:T(8,128)(2,1)}, bf16[128,1024]{1,0:T(8,128)(2,1)}, bf16[128,512]{1,0:T(8,128)(2,1)}, bf16[64,128]{1,0:T(8,128)(2,1)}) custom-call(bf16[128,2048]{1,0:T(8,128)(2,1)} %get-tuple-element.15.refs_0_, bf16[128,2048]{1,0:T(8,128)(2,1)} %get-tuple-element.16.refs_1_, ...), custom_call_target="tpu_custom_call" | custom-call | tf_op jit(solution)/shard_map/pallas_call | solution.py:555

commit v5 on v4

--- a/solution.py
+++ b/solution.py
@@ -354,8 +354,9 @@
     blocks = ROWS // BLOCK
     share_window(0)
     await_window(0)
-    attend_from(0, 0, blocks)
+    attend_from(0, 0, 1)
     share_window(1)
+    attend_from(0, 1, blocks)
     for h in range(2):
         key_grads(0, h)
         share_grads(0, h)

time: 70.2 us -> 69.8 us (level)
  no operation moved by 1% of the time
where the time goes in v5:
time: 69.8 us; the launch traced here: 69.7 us
  Pallas kernels  69.1 us (99%)
    pallas_call x1, Pallas kernels, local(): pl.pallas_call(kernel, out_shape=shapes, in_specs=[hbm] * 9, out_specs=(h...  66.9 us
    pallas_call x1, Pallas kernels, local(): pl.pallas_call(copy_kernel, out_shape=shapes, in_specs=[hbm] * 5, out_spe...  2.22 us

profile of v5, /device:TPU:1, one launch (start us, length us, event | category | flops | bytes accessed | tf_op | source)
XLA Modules:
  0.0 69.7 jit_solution(12565990496408265946)
XLA Ops:
  0.6 66.9 %shard_map.128 = (bf16[128,2048]{1,0:T(8,128)(2,1)}, bf16[128,2048]{1,0:T(8,128)(2,1)}, bf16[128,1024]{1,0:T(8,128)(2,1)}, bf16[128,512]{1,0:T(8,128)(2,1)}, bf16[64,128]{1,0:T(8,128)(2,1)}) custom-call(bf16[128,2048]{1,0:T(8,128)(2,1)} %qn_hbm.1, bf16[128,1024]{1,0:T(8,128)(2,1)} %qr_hbm.1, bf16[128,512]{1,0:T(8,128)(2,1)} %lat_hbm.1, ...), custom_call_target="tpu_custom_call" | custom-call | tf_op jit(solution)/shard_map/pallas_call | solution.py:543
  67.5 2.2 %shard_map.129 = (bf16[128,2048]{1,0:T(8,128)(2,1)}, bf16[128,2048]{1,0:T(8,128)(2,1)}, bf16[128,1024]{1,0:T(8,128)(2,1)}, bf16[128,512]{1,0:T(8,128)(2,1)}, bf16[64,128]{1,0:T(8,128)(2,1)}) custom-call(bf16[128,2048]{1,0:T(8,128)(2,1)} %get-tuple-element.15.refs_0_, bf16[128,2048]{1,0:T(8,128)(2,1)} %get-tuple-element.16.refs_1_, ...), custom_call_target="tpu_custom_call" | custom-call | tf_op jit(solution)/shard_map/pallas_call | solution.py:556
